TPU v7x, 32 devices: a whole 2x2x4 slice. The times are simulated.
32 devices in a mesh: dp: 16 (over z, y, x), mp: 2 (over core).
Axes of the slice: x: 2, y: 2, z: 4, core: 2. Of those that a mesh axis runs over, the one named last changes fastest.
Arguments:
- inputs: bfloat16 [16384, 1024], P(('dp', 'mp'))
- cotangent: bfloat16 [16384, 1024], P(('dp', 'mp')), may hold values from -6 to 6
- lengths: int32 [16, 4], P('dp'), may hold values from 64 to 512, as said below
- seq_order: int32 [16, 4], P('dp'), may hold values from 0 to 3, as said below
- w_qkv: bfloat16 [2, 3, 1024, 1024], P(None, None, 'dp', 'mp'), may hold values from -0.1875 to 0.1875
- w_out: bfloat16 [2, 1024, 1024], P(None, 'mp', 'dp'), may hold values from -1.5 to 1.5
- w_in: bfloat16 [2, 1024, 4096], P(None, 'dp', 'mp'), may hold values from -0.1875 to 0.1875
- w_back: bfloat16 [2, 4096, 1024], P(None, 'mp', 'dp'), may hold values from -0.09375 to 0.09375
- biases: bfloat16 [2, 6, 1024], P(None, None, 'dp'), may hold values from -2 to 2
- norm_gains: bfloat16 [2, 2, 1024], P(None, None, 'dp'), may hold values from 0.5 to 1.5
- hidden_bias: bfloat16 [2, 4, 1024], P(None, 'mp', 'dp'), may hold values from -2 to 2
Outputs:
- output: bfloat16 [16384, 1024], P(('dp', 'mp'))
- input_grad: float32 [16384, 1024], P(('dp', 'mp'))
- grad_qkv: float32 [2, 3, 1024, 1024], P(None, None, 'dp', 'mp')
- grad_out: float32 [2, 1024, 1024], P(None, 'mp', 'dp')
- grad_in: float32 [2, 1024, 4096], P(None, 'dp', 'mp')
- grad_back: float32 [2, 4096, 1024], P(None, 'mp', 'dp')
- grad_biases: float32 [2, 6, 1024], P(None, None, 'dp')
- grad_gains: float32 [2, 2, 1024], P(None, None, 'dp')
- grad_hidden_bias: float32 [2, 4, 1024], P(None, 'mp', 'dp')
- rms: float32 [2, 3], replicated
Inputs may be any that keep to these rules, and one draw needn't show every extreme that they name: Each group's lengths sum to at most 1024; the sequence at place 2 of each group's balanced order has exactly 512 tokens. Each row of seq_order is a permutation of 0 to 3.
All inputs are finite; a program needn't handle non-finite values.
Results may differ from a plain program's by a relative error of at most 0.035.
Values may be sent and summed in bfloat16 or wider, within the bound.
A program may use at most 320 MiB of HBM per device.

v0:
```python
import jax
import jax.numpy as jnp
from jax import lax
from jax.sharding import PartitionSpec as P

HEADS = 16
HEAD_DIM = 64
LAYERS = 2


layer_eps = 1e-12
half_root = 0.7071067811865476
density_scale = 0.3989422804014327


def plan_rows(lengths, seq_order, total_rows):
    count = lengths.shape[0]
    labels = jnp.arange(count, dtype=jnp.int32)
    picked = (seq_order[:, None] == labels[None, :]).astype(jnp.int32)
    bal_len = jnp.sum(picked * lengths[None, :], axis=1)
    bal_end = jnp.cumsum(bal_len)
    bal_start = bal_end - bal_len
    giv_end = jnp.cumsum(lengths)
    giv_start = giv_end - lengths
    row_ids = jnp.arange(total_rows, dtype=jnp.int32)
    bal_seg = jnp.sum((bal_end[None, :] <= row_ids[:, None]).astype(jnp.int32), axis=1)
    giv_seg = jnp.sum((giv_end[None, :] <= row_ids[:, None]).astype(jnp.int32), axis=1)
    shift_seq = jnp.sum(picked * bal_start[:, None], axis=0) - giv_start
    giv_hit = (giv_seg[:, None] == labels[None, :]).astype(jnp.int32)
    source = row_ids + jnp.sum(giv_hit * shift_seq[None, :], axis=1)
    shift_pos = bal_start - jnp.sum(picked * giv_start[None, :], axis=1)
    bal_hit = (bal_seg[:, None] == labels[None, :]).astype(jnp.int32)
    target = row_ids - jnp.sum(bal_hit * shift_pos[None, :], axis=1)
    return (bal_seg, giv_seg, source, target)


def matmul(left_mat, right_mat):
    return jnp.dot(left_mat, right_mat, preferred_element_type=jnp.float32)


def left_t(left_mat, right_mat):
    return lax.dot_general(
        left_mat, right_mat, (((0,), (0,)), ((), ())), preferred_element_type=jnp.float32
    )


def right_t(left_mat, right_mat):
    return lax.dot_general(
        left_mat, right_mat, (((1,), (1,)), ((), ())), preferred_element_type=jnp.float32
    )


def gelu_value(values):
    return 0.5 * values * (1.0 + lax.erf(values * half_root))


def gelu_slope(values):
    return 0.5 * (1.0 + lax.erf(values * half_root)) + values * density_scale * jnp.exp(
        -0.5 * values * values
    )


def norm_rows(values, gain_vec, shift_vec):
    center = values - jnp.mean(values, axis=-1, keepdims=True)
    inv_scale = lax.rsqrt(jnp.mean(center * center, axis=-1, keepdims=True) + layer_eps)
    unit_rows = center * inv_scale
    return (unit_rows * gain_vec + shift_vec, unit_rows, inv_scale)


def norm_back(grad_rows, unit_rows, inv_scale, gain_vec):
    scaled = grad_rows * gain_vec
    inner_part = (
        scaled
        - jnp.mean(scaled, axis=-1, keepdims=True)
        - unit_rows * jnp.mean(scaled * unit_rows, axis=-1, keepdims=True)
    )
    return (
        inner_part * inv_scale,
        jnp.sum(grad_rows * unit_rows, axis=0),
        jnp.sum(grad_rows, axis=0),
    )


def gather_rows(values):
    return lax.all_gather(values, "mp", axis=0, tiled=True)


def sum_rows(values):
    return lax.psum_scatter(
        values.astype(jnp.bfloat16), "mp", scatter_dimension=0, tiled=True
    ).astype(jnp.float32)


def gather_grads(values):
    return lax.all_gather(values, "mp", axis=0, tiled=True)


def sum_grads(values):
    return lax.psum_scatter(
        values.astype(jnp.bfloat16), "mp", scatter_dimension=0, tiled=True
    ).astype(jnp.float32)


def fetch_forward(w_qkv, w_out, w_in, w_back, biases, norm_gains, hidden_bias, layer_idx):
    return (
        lax.all_gather(w_qkv[layer_idx], "dp", axis=1, tiled=True),
        lax.all_gather(w_out[layer_idx], "dp", axis=1, tiled=True),
        lax.all_gather(w_in[layer_idx], "dp", axis=0, tiled=True),
        lax.all_gather(w_back[layer_idx], "dp", axis=1, tiled=True),
        lax.all_gather(biases[layer_idx], "dp", axis=1, tiled=True),
        lax.all_gather(norm_gains[layer_idx], "dp", axis=1, tiled=True),
        lax.all_gather(hidden_bias[layer_idx], "dp", axis=1, tiled=True),
    )


def fetch_backward(w_qkv, w_out, w_in, w_back, biases, norm_gains, hidden_bias, layer_idx):
    return (
        lax.all_gather(w_qkv[layer_idx], "dp", axis=1, tiled=True),
        lax.all_gather(w_out[layer_idx], "dp", axis=1, tiled=True),
        lax.all_gather(w_in[layer_idx], "dp", axis=0, tiled=True),
        lax.all_gather(w_back[layer_idx], "dp", axis=1, tiled=True),
        lax.all_gather(biases[layer_idx], "dp", axis=1, tiled=True),
        lax.all_gather(norm_gains[layer_idx], "dp", axis=1, tiled=True),
        lax.all_gather(hidden_bias[layer_idx], "dp", axis=1, tiled=True),
    )


def split_heads(values, heads_here):
    return values.reshape(values.shape[0], heads_here, values.shape[1] // heads_here)


def attend(queries, key_rows, values, same_seq, heads_here, score_scale):
    query_heads = split_heads(queries, heads_here)
    key_heads = split_heads(key_rows, heads_here)
    value_heads = split_heads(values, heads_here)
    scores = (
        jnp.einsum("qhd,khd->hqk", query_heads, key_heads, preferred_element_type=jnp.float32)
        * score_scale
    )
    masked = jnp.where(same_seq[None], scores, -1e30)
    peak = jnp.max(masked, axis=-1, keepdims=True)
    shifted = jnp.exp(masked - peak)
    totals = jnp.sum(shifted, axis=-1, keepdims=True)
    weights_low = (shifted / totals).astype(jnp.bfloat16)
    mixture = jnp.einsum(
        "hqk,khd->qhd", weights_low, value_heads, preferred_element_type=jnp.float32
    )
    return (mixture.reshape(queries.shape[0], -1), peak + jnp.log(totals))


def attend_back(queries, key_rows, values, log_total, grad_mix, same_seq, heads_here, score_scale):
    row_count = queries.shape[0]
    query_heads = split_heads(queries, heads_here)
    key_heads = split_heads(key_rows, heads_here)
    value_heads = split_heads(values, heads_here)
    grad_heads = split_heads(grad_mix, heads_here)
    scores = (
        jnp.einsum("qhd,khd->hqk", query_heads, key_heads, preferred_element_type=jnp.float32)
        * score_scale
    )
    masked = jnp.where(same_seq[None], scores, -1e30)
    probs = jnp.exp(masked - log_total)
    grad_probs = jnp.einsum(
        "qhd,khd->hqk", grad_heads, value_heads, preferred_element_type=jnp.float32
    )
    inner_sum = jnp.sum(probs * grad_probs, axis=-1, keepdims=True)
    grad_scores = (probs * (grad_probs - inner_sum)).astype(jnp.bfloat16)
    grad_query = (
        jnp.einsum("hqk,khd->qhd", grad_scores, key_heads, preferred_element_type=jnp.float32)
        * score_scale
    ).astype(jnp.bfloat16)
    grad_key = (
        jnp.einsum("hqk,qhd->khd", grad_scores, query_heads, preferred_element_type=jnp.float32)
        * score_scale
    ).astype(jnp.bfloat16)
    grad_value = jnp.einsum(
        "hqk,qhd->khd", probs.astype(jnp.bfloat16), grad_heads, preferred_element_type=jnp.float32
    ).astype(jnp.bfloat16)
    return jnp.stack(
        [
            grad_query.reshape(row_count, -1),
            grad_key.reshape(row_count, -1),
            grad_value.reshape(row_count, -1),
        ]
    )


def forward_layer(stream, fetched, same_seq, part_index, heads_here, score_scale):
    w_proj, w_mix, w_up, w_down, bias_rows, gain_rows, hidden_rows = fetched
    head_cols = w_proj.shape[2]
    bias_all = bias_rows.astype(jnp.float32)
    gain_all = gain_rows.astype(jnp.float32)
    stream_all = gather_rows(stream.astype(jnp.bfloat16))
    projected = jnp.einsum("rd,tdc->trc", stream_all, w_proj, preferred_element_type=jnp.float32)
    query_bias = lax.dynamic_slice_in_dim(bias_all[0], part_index * head_cols, head_cols)
    value_bias = lax.dynamic_slice_in_dim(bias_all[1], part_index * head_cols, head_cols)
    queries = (projected[0] + query_bias).astype(jnp.bfloat16)
    key_rows = projected[1].astype(jnp.bfloat16)
    values = (projected[2] + value_bias).astype(jnp.bfloat16)
    mixture, log_total = attend(queries, key_rows, values, same_seq, heads_here, score_scale)
    mix_low = mixture.astype(jnp.bfloat16)
    branch = sum_rows(matmul(mix_low, w_mix)) + bias_all[2]
    normed, unit_one, inv_one = norm_rows(stream + branch, gain_all[0], bias_all[3])
    normed_all = gather_rows(normed.astype(jnp.bfloat16))
    hidden = matmul(normed_all, w_up) + hidden_rows.reshape(-1).astype(jnp.float32)
    active = gelu_value(hidden).astype(jnp.bfloat16)
    second = sum_rows(matmul(active, w_down)) + bias_all[4]
    result, unit_two, inv_two = norm_rows(normed + second, gain_all[1], bias_all[5])
    saved = (
        stream_all,
        queries,
        key_rows,
        values,
        log_total,
        mix_low,
        unit_one,
        inv_one,
        normed_all,
        hidden,
        active,
        unit_two,
        inv_two,
    )
    return (saved, result, branch, second)


def backward_layer(grad_stream, fetched, saved, same_seq, part_index, heads_here, score_scale):
    w_proj, w_mix, w_up, w_down, bias_rows, gain_rows, hidden_rows = fetched
    (
        stream_all,
        queries,
        key_rows,
        values,
        log_total,
        mix_low,
        unit_one,
        inv_one,
        normed_all,
        hidden,
        active,
        unit_two,
        inv_two,
    ) = saved
    width = w_mix.shape[1]
    head_cols = w_proj.shape[2]
    gain_all = gain_rows.astype(jnp.float32)
    grad_mid, gain_two, shift_two = norm_back(grad_stream, unit_two, inv_two, gain_all[1])
    grad_second = grad_mid.astype(jnp.bfloat16)
    second_bias = jnp.sum(grad_second.astype(jnp.float32), axis=0)
    second_all = gather_grads(grad_second)
    down_grad = left_t(active, second_all)
    grad_hidden = (right_t(second_all, w_down) * gelu_slope(hidden)).astype(jnp.bfloat16)
    hidden_grad = jnp.sum(grad_hidden.astype(jnp.float32), axis=0).reshape(hidden_rows.shape)
    up_grad = left_t(normed_all, grad_hidden)
    grad_normed = grad_mid + sum_grads(right_t(grad_hidden, w_up))
    grad_first, gain_one, shift_one = norm_back(grad_normed, unit_one, inv_one, gain_all[0])
    grad_branch = grad_first.astype(jnp.bfloat16)
    branch_bias = jnp.sum(grad_branch.astype(jnp.float32), axis=0)
    branch_all = gather_grads(grad_branch)
    mix_grad = left_t(mix_low, branch_all)
    grad_mix = right_t(branch_all, w_mix).astype(jnp.bfloat16)
    grad_proj = attend_back(
        queries, key_rows, values, log_total, grad_mix, same_seq, heads_here, score_scale
    )
    proj_grad = jnp.einsum("rd,trc->tdc", stream_all, grad_proj, preferred_element_type=jnp.float32)
    proj_sums = jnp.sum(grad_proj.astype(jnp.float32), axis=1)
    empty_vec = jnp.zeros((width,), jnp.float32)
    query_bias = lax.dynamic_update_slice_in_dim(empty_vec, proj_sums[0], part_index * head_cols, 0)
    value_bias = lax.dynamic_update_slice_in_dim(empty_vec, proj_sums[2], part_index * head_cols, 0)
    grad_input = grad_first + sum_grads(
        jnp.einsum("trc,tdc->rd", grad_proj, w_proj, preferred_element_type=jnp.float32)
    )
    bias_grad = jnp.stack([query_bias, value_bias, branch_bias, shift_one, second_bias, shift_two])
    gain_grad = jnp.stack([gain_one, gain_two])
    return (
        grad_input,
        (proj_grad, mix_grad, up_grad, down_grad, hidden_grad),
        bias_grad,
        gain_grad,
    )


def body(
    inputs,
    cotangent,
    lengths,
    seq_order,
    w_qkv,
    w_out,
    w_in,
    w_back,
    biases,
    norm_gains,
    hidden_bias,
):
    part_count = lax.axis_size("mp")
    part_index = lax.axis_index("mp")
    own_count = inputs.shape[0]
    width = inputs.shape[1]
    group_rows = own_count * part_count
    seq_count = lengths.shape[1]
    heads_here = HEADS // part_count
    score_scale = HEAD_DIM ** (-0.5)
    bal_seg, giv_seg, source, target = plan_rows(lengths[0], seq_order[0], group_rows)
    same_seq = bal_seg[:, None] == bal_seg[None, :]
    row_start = part_index * own_count
    own_bal = lax.dynamic_slice_in_dim(bal_seg, row_start, own_count)
    own_giv = lax.dynamic_slice_in_dim(giv_seg, row_start, own_count)
    valid_rows = (own_bal < seq_count).astype(jnp.float32)[:, None]
    given_valid = own_giv < seq_count
    stream = inputs.astype(jnp.float32)
    kept_layers = []
    square_rows = []
    for layer_idx in range(LAYERS):
        fetched = fetch_forward(
            w_qkv, w_out, w_in, w_back, biases, norm_gains, hidden_bias, layer_idx
        )
        saved, result, branch, second = forward_layer(
            stream, fetched, same_seq, part_index, heads_here, score_scale
        )
        square_rows.append(
            jnp.stack(
                [
                    jnp.sum(valid_rows * stream * stream),
                    jnp.sum(valid_rows * branch * branch),
                    jnp.sum(valid_rows * second * second),
                ]
            )
        )
        kept_layers.append((fetched, saved))
        stream = result
    out_low = stream.astype(jnp.bfloat16)
    out_all, cot_all = (
        lax.all_gather(out_low, "mp", axis=0, tiled=True),
        lax.all_gather(cotangent, "mp", axis=0, tiled=True),
    )
    own_source = lax.dynamic_slice_in_dim(source, row_start, own_count)
    own_target = lax.dynamic_slice_in_dim(target, row_start, own_count)
    output = jnp.where(given_valid[:, None], out_all[own_source], jnp.zeros((), jnp.bfloat16))
    grad_stream = cot_all[own_target].astype(jnp.float32) * valid_rows
    weight_terms = [None] * LAYERS
    bias_terms = [None] * LAYERS
    gain_terms = [None] * LAYERS
    for layer_idx in reversed(range(LAYERS)):
        fetched, saved = kept_layers[layer_idx]
        fetched = fetch_backward(
            w_qkv, w_out, w_in, w_back, biases, norm_gains, hidden_bias, layer_idx
        )
        grad_stream, mats, bias_grad, gain_grad = backward_layer(
            grad_stream, fetched, saved, same_seq, part_index, heads_here, score_scale
        )
        bias_terms[layer_idx] = bias_grad
        gain_terms[layer_idx] = gain_grad
        weight_terms[layer_idx] = (
            lax.psum_scatter(mats[0], "dp", scatter_dimension=1, tiled=True),
            lax.psum_scatter(mats[1], "dp", scatter_dimension=1, tiled=True),
            lax.psum_scatter(mats[2], "dp", scatter_dimension=0, tiled=True),
            lax.psum_scatter(mats[3], "dp", scatter_dimension=1, tiled=True),
            lax.psum_scatter(mats[4], "dp", scatter_dimension=1, tiled=True),
        )
    stacked = tuple((jnp.stack([terms[member] for terms in weight_terms]) for member in range(5)))
    sums_sq, count_all, bias_sum, gain_sum = lax.psum(
        (jnp.stack(square_rows), jnp.sum(valid_rows), jnp.stack(bias_terms), jnp.stack(gain_terms)),
        ("dp", "mp"),
    )
    span_cols = width // lax.axis_size("dp")
    dp_start = lax.axis_index("dp") * span_cols
    grad_biases = lax.dynamic_slice_in_dim(bias_sum, dp_start, span_cols, 2)
    grad_gains = lax.dynamic_slice_in_dim(gain_sum, dp_start, span_cols, 2)
    rms = jnp.sqrt(sums_sq / (count_all * width))
    return (
        output,
        grad_stream,
        stacked[0],
        stacked[1],
        stacked[2],
        stacked[3],
        grad_biases,
        grad_gains,
        stacked[4],
        rms,
    )


def solution(mesh):
    in_specs = (
        P(("dp", "mp"), None),
        P(("dp", "mp"), None),
        P("dp", None),
        P("dp", None),
        P(None, None, "dp", "mp"),
        P(None, "mp", "dp"),
        P(None, "dp", "mp"),
        P(None, "mp", "dp"),
        P(None, None, "dp"),
        P(None, None, "dp"),
        P(None, "mp", "dp"),
    )
    out_specs = (
        P(("dp", "mp"), None),
        P(("dp", "mp"), None),
        P(None, None, "dp", "mp"),
        P(None, "mp", "dp"),
        P(None, "dp", "mp"),
        P(None, "mp", "dp"),
        P(None, None, "dp"),
        P(None, None, "dp"),
        P(None, "mp", "dp"),
        P(),
    )
    return jax.shard_map(body, mesh=mesh, in_specs=in_specs, out_specs=out_specs, check_vma=False)
```

profile of v0, /device:TPU:0, one launch (start us, length us, event | category | flops | bytes accessed | tf_op | source)
XLA Modules:
  0.0 2515.7 jit_solution(720589894329100405)
XLA Ops:
  11.6 45.5 %all-gather.1 = bf16[1,6,1024]{1,0,2:T(2,128)(2,1)S(1)} all-gather(bf16[1,6,64]{1,0,2:T(2,128)(2,1)S(1)} %copy.211), channel_id=3, replica_groups=mesh['dp'=16,'mp'=2] {'dp'}, dimensions={2}, use_global_device_ids=true | all-gather | bytes 13056 | tf_op jit(solution)/shard_map/all_gather | solution.py:110
  61.7 33.8 %all-gather.53.cloned.1.call-done = bf16[1,3,1024,512]{3,2,1,0:T(8,128)(2,1)} async-done(((bf16[1,3,64,512]{3,2,1,0:T(8,128)(2,1)}), bf16[1,3,1024,512]{3,2,1,0:T(8,128)(2,1)}) %all-gather.53.cloned.1.call-update) | async-done | bytes 3145744 | tf_op jit(solution)/shard_map/all_gather | solution.py:106
  102.7 13.9 fusion.124
  116.5 13.1 fusion
  130.2 14.9 fusion.93
  160.0 42.2 %all-gather.3 = bf16[1,2,1024]{1,0,2:T(2,128)(2,1)S(1)} all-gather(bf16[1,2,64]{1,0,2:T(2,128)(2,1)S(1)} %copy.212), channel_id=5, replica_groups=mesh['dp'=16,'mp'=2] {'dp'}, dimensions={2}, use_global_device_ids=true | all-gather | bytes 4352 | tf_op jit(solution)/shard_map/all_gather | solution.py:111
  208.9 20.9 slice_reduce_fusion.6
  235.9 41.7 %all-gather.5 = bf16[1,2,1024]{1,0,2:T(2,128)(2,1)} all-gather(bf16[1,2,64]{1,0,2:T(2,128)(2,1)S(1)} %copy.213), channel_id=7, replica_groups=mesh['dp'=16,'mp'=2] {'dp'}, dimensions={2}, use_global_device_ids=true | all-gather | bytes 4352 | tf_op jit(solution)/shard_map/all_gather | solution.py:112
  289.2 53.9 %all-gather.59.cloned.1.call-done = bf16[1,2048,1024]{1,2,0:T(8,128)(2,1)} async-done(((bf16[1,2048,64]{1,2,0:T(8,128)(2,1)}), bf16[1,2048,1024]{1,2,0:T(8,128)(2,1)}) %all-gather.59.cloned.1.call-update) | async-done | bytes 4194320 | tf_op jit(solution)/shard_map/all_gather | solution.py:109
  370.8 45.0 %all-gather.8 = bf16[1,6,1024]{1,0,2:T(2,128)(2,1)S(1)} all-gather(bf16[1,6,64]{1,0,2:T(2,128)(2,1)S(1)} %copy.214), channel_id=10, replica_groups=mesh['dp'=16,'mp'=2] {'dp'}, dimensions={2}, use_global_device_ids=true | all-gather | bytes 13056 | tf_op jit(solution)/shard_map/all_gather | solution.py:110
  419.7 15.6 all-gather.61.cloned.1.call-done
  454.3 13.9 fusion.125
  468.2 13.1 fusion.1
  481.3 13.8 fusion.92
  511.7 42.2 %all-gather.10 = bf16[1,2,1024]{1,0,2:T(2,128)(2,1)S(1)} all-gather(bf16[1,2,64]{1,0,2:T(2,128)(2,1)S(1)} %copy.215), channel_id=12, replica_groups=mesh['dp'=16,'mp'=2] {'dp'}, dimensions={2}, use_global_device_ids=true | all-gather | bytes 4352 | tf_op jit(solution)/shard_map/all_gather | solution.py:111
  560.7 20.6 slice_reduce_fusion
  586.8 39.5 %all-gather.12 = bf16[1,2,1024]{1,0,2:T(2,128)(2,1)S(1)} all-gather(bf16[1,2,64]{1,0,2:T(2,128)(2,1)S(1)} %copy.216), channel_id=14, replica_groups=mesh['dp'=16,'mp'=2] {'dp'}, dimensions={2}, use_global_device_ids=true | all-gather | bytes 4352 | tf_op jit(solution)/shard_map/all_gather | solution.py:112
  637.1 60.8 %all-gather.67.cloned.1.call-done = bf16[1,2048,1024]{1,2,0:T(8,128)(2,1)} async-done(((bf16[1,2048,64]{1,2,0:T(8,128)(2,1)}), bf16[1,2048,1024]{1,2,0:T(8,128)(2,1)}) %all-gather.67.cloned.1.call-update) | async-done | bytes 4194320 | tf_op jit(solution)/shard_map/all_gather | solution.py:109
  792.4 14.6 fusion.86
  807.0 21.7 multiply_reduce_fusion.1
  828.7 28.7 %multiply_convert_fusion.1 = bf16[8,1024,1024]{1,2,0:T(8,128)(2,1)} fusion(f32[8,1024,1024]{1,2,0:T(8,128)} %get-tuple-element.165, f32[8,1024,1024]{1,2,0:T(8,128)} %get-tuple-element.161, f32[8,1024]{1,0:T(8,128)S(1)} %get-tuple-element.164, f32[8,1024]{1,0:T(8,128)S(1)} %log_add_fusion.1), kind=kLoop, calls=%fused_computation.5 | loop fusion | flops 33554432 | bytes 83951616 | tf_op jit(solution)/shard_map/convert_element_type | solution.py:167
  857.5 12.1 multiply_convert_fusion.6
  978.4 23.0 multiply_reduce_fusion
  1001.4 28.3 %multiply_convert_fusion = bf16[8,1024,1024]{1,2,0:T(8,128)(2,1)} fusion(f32[8,1024,1024]{1,2,0:T(8,128)} %get-tuple-element.167, f32[8,1024,1024]{1,2,0:T(8,128)} %get-tuple-element.157, f32[8,1024]{1,0:T(8,128)S(1)} %get-tuple-element.166, f32[8,1024]{1,0:T(8,128)S(1)} %log_add_fusion), kind=kLoop, calls=%fused_computation.2 | loop fusion | flops 33554432 | bytes 83951616 | tf_op jit(solution)/shard_map/convert_element_type | solution.py:167
  1029.7 13.4 fusion.89
  1174.8 43.1 %all-reduce.8 = (f32[2,6,1024]{2,1,0:T(8,128)S(1)}, f32[2,2,1024]{2,1,0:T(2,128)S(1)}, f32[2,3]{1,0:T(2,128)S(1)}, f32[]{:T(128)}) all-reduce(f32[2,6,1024]{2,1,0:T(8,128)S(1)} %pad_maximum_fusion.6, f32[2,2,1024]{2,1,0:T(2,128)S(1)} %pad_maximum_fusion.7, ...), channel_id=1, replica_groups=mesh['dp'=16,'mp'=2] {'dp','mp'}, use_global_device_ids=true, to_apply=%region_57.58 | all-reduce | flops 16391 | bytes 131128 | tf_op jit(solution)/shard_map/psum | solution.py:362
  1220.5 79.6 %reduce-scatter.37.cloned.1.call-done = f32[512,64]{0,1:T(8,128)} async-done(((f32[512,1024]{0,1:T(8,128)}), f32[512,64]{0,1:T(8,128)}) %reduce-scatter.37.cloned.1.call-update) | async-done | bytes 131088 | tf_op jit(solution)/shard_map/reduce_scatter | solution.py:356
  1312.0 178.5 %reduce-scatter.47.cloned.1.call-done = f32[2048,64]{0,1:T(8,128)} async-done(((f32[2048,1024]{0,1:T(8,128)}), f32[2048,64]{0,1:T(8,128)}) %reduce-scatter.47.cloned.1.call-update) | async-done | bytes 524304 | tf_op jit(solution)/shard_map/reduce_scatter | solution.py:358
  1490.5 182.6 %reduce-scatter.45.cloned.1.call-done = f32[2048,64]{0,1:T(8,128)} async-done(((f32[2048,1024]{0,1:T(8,128)}), f32[2048,64]{0,1:T(8,128)}) %reduce-scatter.45.cloned.1.call-update) | async-done | bytes 524304 | tf_op jit(solution)/shard_map/reduce_scatter | solution.py:358
  1675.4 180.1 %reduce-scatter.43.cloned.1.call-done = f32[64,2048]{1,0:T(8,128)} async-done(((f32[1024,2048]{1,0:T(8,128)}), f32[64,2048]{1,0:T(8,128)}) %reduce-scatter.43.cloned.1.call-update) | async-done | bytes 524304 | tf_op jit(solution)/shard_map/reduce_scatter | solution.py:357
  1855.5 182.6 %reduce-scatter.41.cloned.1.call-done = f32[64,2048]{1,0:T(8,128)} async-done(((f32[1024,2048]{1,0:T(8,128)}), f32[64,2048]{1,0:T(8,128)}) %reduce-scatter.41.cloned.1.call-update) | async-done | bytes 524304 | tf_op jit(solution)/shard_map/reduce_scatter | solution.py:357
  2040.3 464.7 %all-reduce.7.cloned.1.call-done = (f32[3,1024,512]{2,0,1:T(4,128)}, f32[3,1024,512]{2,0,1:T(4,128)}) async-done(((f32[3,1024,512]{2,0,1:T(4,128)}, f32[3,1024,512]{2,0,1:T(4,128)}), (f32[3,1024,512]{2,0,1:T(4,128)}, f32[3,1024,512]{2,0,1:T(4,128)})) %all-reduce.7.cloned.1.call-update) | async-done | bytes 12582928
  (470 shorter events, 500.9 us)
Async XLA Ops:
  7.2 54.4 %all-gather.33.cloned.1.call-start = ((), (), s32[]{:S(2)}) async-start(), calls=%async_computation.16 | async-start | bytes 3145728 | tf_op jit(solution)/shard_map/all_gather | solution.py:85
  8.0 87.5 %all-gather.53.cloned.1.call-start = ((), (), s32[]{:S(2)}) async-start(), calls=%async_computation.40 | async-start | bytes 3342336 | tf_op jit(solution)/shard_map/all_gather | solution.py:106
  9.8 143.3 %all-gather.55.cloned.1.call-start = ((), (), s32[]{:S(2)}) async-start(), calls=%async_computation.41 | async-start | bytes 1114112 | tf_op jit(solution)/shard_map/all_gather | solution.py:107
  10.6 219.3 %reduce-scatter.21.cloned.1.call-start = ((), (), s32[]{:S(2)}) async-start(), calls=%async_computation.17 | async-start | bytes 3145728 | tf_op jit(solution)/shard_map/reduce_scatter | solution.py:89
  157.4 121.7 %all-gather.57.cloned.1.call-start = ((), (), s32[]{:S(2)}) async-start(), calls=%async_computation.42 | async-start | bytes 4456448 | tf_op jit(solution)/shard_map/all_gather | solution.py:108
  159.2 119.8 %all-gather.35.cloned.1.call-start = ((), (), s32[]{:S(2)}) async-start(), calls=%async_computation.18 | async-start | bytes 3145728 | tf_op jit(solution)/shard_map/all_gather | solution.py:85
  233.8 109.4 %all-gather.59.cloned.1.call-start = ((), (), s32[]{:S(2)}) async-start(), calls=%async_computation.43 | async-start | bytes 4456448 | tf_op jit(solution)/shard_map/all_gather | solution.py:109
  235.7 125.1 %reduce-scatter.23.cloned.1.call-start = ((), (), s32[]{:S(2)}) async-start(), calls=%async_computation.19 | async-start | bytes 3145728 | tf_op jit(solution)/shard_map/reduce_scatter | solution.py:89
  352.5 82.8 %all-gather.61.cloned.1.call-start = ((), (), s32[]{:S(2)}) async-start(), calls=%async_computation.44 | async-start | bytes 3342336 | tf_op jit(solution)/shard_map/all_gather | solution.py:106
  353.2 93.8 %all-gather.37.cloned.1.call-start = ((), (), s32[]{:S(2)}) async-start(), calls=%async_computation.20 | async-start | bytes 3145728 | tf_op jit(solution)/shard_map/all_gather | solution.py:85
  369.9 136.4 %all-gather.63.cloned.1.call-start = ((), (), s32[]{:S(2)}) async-start(), calls=%async_computation.45 | async-start | bytes 1114112 | tf_op jit(solution)/shard_map/all_gather | solution.py:107
  370.6 210.6 %reduce-scatter.25.cloned.1.call-start = ((), (), s32[]{:S(2)}) async-start(), calls=%async_computation.21 | async-start | bytes 3145728 | tf_op jit(solution)/shard_map/reduce_scatter | solution.py:89
  510.2 116.7 %all-gather.65.cloned.1.call-start = ((), (), s32[]{:S(2)}) async-start(), calls=%async_computation.46 | async-start | bytes 4456448 | tf_op jit(solution)/shard_map/all_gather | solution.py:108
  511.0 115.9 %all-gather.39.cloned.1.call-start = ((), (), s32[]{:S(2)}) async-start(), calls=%async_computation.22 | async-start | bytes 3145728 | tf_op jit(solution)/shard_map/all_gather | solution.py:85
  585.5 112.4 %all-gather.67.cloned.1.call-start = ((), (), s32[]{:S(2)}) async-start(), calls=%async_computation.47 | async-start | bytes 4456448 | tf_op jit(solution)/shard_map/all_gather | solution.py:109
  586.1 122.8 %all-gather.43.cloned.1.call-start = ((), (), s32[]{:S(2)}) async-start(), calls=%async_computation.25 | async-start | bytes 3145728 | tf_op jit(solution)/shard_map/all_gather | solution.py:335
  586.6 135.0 %reduce-scatter.27.cloned.1.call-start = ((), (), s32[]{:S(2)}) async-start(), calls=%async_computation.23 | async-start | bytes 3145728 | tf_op jit(solution)/shard_map/reduce_scatter | solution.py:89
  707.3 33.4 %all-gather.45.cloned.1.call-start = ((), (), s32[]{:S(2)}) async-start(), calls=%async_computation.26 | async-start | bytes 3145728 | tf_op jit(solution)/shard_map/all_gather | solution.py:95
  728.8 41.9 %reduce-scatter.29.cloned.1.call-start = ((), (), s32[]{:S(2)}) async-start(), calls=%async_computation.27 | async-start | bytes 3145728 | tf_op jit(solution)/shard_map/reduce_scatter | solution.py:99
  777.3 125.1 %reduce-scatter.31.cloned.1.call-start = ((), (), s32[]{:S(2)}) async-start(), calls=%async_computation.29 | async-start | bytes 3145728 | tf_op jit(solution)/shard_map/reduce_scatter | solution.py:99
  909.8 41.4 %reduce-scatter.33.cloned.1.call-start = ((), (), s32[]{:S(2)}) async-start(), calls=%async_computation.31 | async-start | bytes 3145728 | tf_op jit(solution)/shard_map/reduce_scatter | solution.py:99
  958.8 199.4 %all-gather.41.cloned.1.call-start = ((), (), s32[]{:S(2)}) async-start(), calls=%async_computation.24 | async-start | bytes 3145728 | tf_op jit(solution)/shard_map/all_gather | solution.py:334
  959.6 204.5 %reduce-scatter.51.cloned.1.call-start = ((), (), s32[]{:S(2)}) async-start(), calls=%async_computation.49 | async-start | bytes 557056
  960.7 208.2 %reduce-scatter.49.cloned.1.call-start = ((), (), s32[]{:S(2)}) async-start(), calls=%async_computation.48 | async-start | bytes 557056
  961.8 258.7 %reduce-scatter.39.cloned.1.call-start = ((), (), s32[]{:S(2)}) async-start(), calls=%async_computation.35 | async-start | bytes 2228224 | tf_op jit(solution)/shard_map/reduce_scatter | solution.py:356
  964.6 335.6 %reduce-scatter.37.cloned.1.call-start = ((), (), s32[]{:S(2)}) async-start(), calls=%async_computation.34 | async-start | bytes 2228224 | tf_op jit(solution)/shard_map/reduce_scatter | solution.py:356
  975.0 334.1 %reduce-scatter.35.cloned.1.call-start = ((), (), s32[]{:S(2)}) async-start(), calls=%async_computation.33 | async-start | bytes 3145728 | tf_op jit(solution)/shard_map/reduce_scatter | solution.py:99
  1077.5 413.0 %reduce-scatter.47.cloned.1.call-start = ((), (), s32[]{:S(2)}) async-start(), calls=%async_computation.39 | async-start | bytes 8912896 | tf_op jit(solution)/shard_map/reduce_scatter | solution.py:358
  1088.1 584.9 %reduce-scatter.45.cloned.1.call-start = ((), (), s32[]{:S(2)}) async-start(), calls=%async_computation.38 | async-start | bytes 8912896 | tf_op jit(solution)/shard_map/reduce_scatter | solution.py:358
  1098.7 756.8 %reduce-scatter.43.cloned.1.call-start = ((), (), s32[]{:S(2)}) async-start(), calls=%async_computation.37 | async-start | bytes 8912896 | tf_op jit(solution)/shard_map/reduce_scatter | solution.py:357
  1109.2 928.8 %reduce-scatter.41.cloned.1.call-start = ((), (), s32[]{:S(2)}) async-start(), calls=%async_computation.36 | async-start | bytes 8912896 | tf_op jit(solution)/shard_map/reduce_scatter | solution.py:357
  1119.8 1385.3 %all-reduce.7.cloned.1.call-start = ((), (), s32[]{:S(2)}) async-start(), calls=%async_computation.50 | async-start | bytes 33554432
  (104 other events, 1576.7 us)
Sparse Core Ops, SparseCore 0:
  9.6 13.2 all-gather.32
  26.2 69.1 all-gather.52
  98.8 54.3 all-gather.54
  157.5 8.4 reduce-scatter.20
  169.5 82.8 all-gather.56
  265.9 77.2 all-gather.58
  363.6 71.6 all-gather.60
  437.3 9.6 all-gather.36
  449.7 56.4 all-gather.62
  510.3 8.3 reduce-scatter.24
  522.5 82.8 all-gather.64
  607.4 9.6 all-gather.38
  620.6 77.2 all-gather.66
  699.4 9.1 all-gather.42
  710.8 10.7 reduce-scatter.26
  728.9 11.7 all-gather.44
  759.8 10.7 reduce-scatter.28
  777.4 11.7 all-gather.46
  891.5 10.7 reduce-scatter.30
  909.9 11.7 all-gather.48
  940.4 10.7 reduce-scatter.32
  959.0 11.7 all-gather.50
  973.0 11.7 all-gather.40
  987.5 77.8 reduce-scatter.50
  1067.5 73.0 reduce-scatter.48
  1143.0 76.9 reduce-scatter.38
  1222.4 77.7 reduce-scatter.36
  1311.4 179.0 reduce-scatter.46
  1492.8 180.2 reduce-scatter.44
  1675.2 180.2 reduce-scatter.42
  1857.8 180.2 reduce-scatter.40
  2044.5 460.5 all-reduce.6
  (3 shorter events, 22.4 us)
where the time goes:
time: 2520 us
  waiting for transfers between devices  1560 us (62%)
  matrix products  345 us (14%)
  blocking collectives  299 us (12%)
  other arithmetic  154 us (6%)
  local copies, waits for them, and re-layouts  135 us (5%)
    unnamed x38, waiting for transfers between devices  470 us
    reduce_scatter x2, waiting for transfers between devices, body(): lax.psum_scatter(mats[2], 'dp', scatter_dimension=0, tiled=True)  363 us
    reduce_scatter x2, waiting for transfers between devices, body(): lax.psum_scatter(mats[3], 'dp', scatter_dimension=1, tiled=True)  361 us
    all_gather x2, waiting for transfers between devices, fetch_forward(): lax.all_gather(w_back[layer_idx], 'dp', axis=1, tiled=True)  115 us
    all_gather x2, blocking collectives, fetch_forward(): lax.all_gather(biases[layer_idx], 'dp', axis=1, tiled=True)  90.5 us
    all_gather x2, blocking collectives, fetch_forward(): lax.all_gather(norm_gains[layer_idx], 'dp', axis=1, tiled=True)  84.5 us
    all_gather x2, blocking collectives, fetch_forward(): lax.all_gather(hidden_bias[layer_idx], 'dp', axis=1, tiled=True)  81.2 us
    reduce_scatter x2, waiting for transfers between devices, body(): lax.psum_scatter(mats[1], 'dp', scatter_dimension=1, tiled=True)  79.7 us
  transfers between devices with their start and end apart: 35, of which 23 were waited for; matrix products, arithmetic and copies ran while one was open for 17% of the time, Pallas kernels for 0%

commit v1 on v0

v1 whole, which is shorter than its diff:
```python
import functools

import jax
import jax.numpy as jnp
from jax import lax
from jax.experimental import pallas as pl
from jax.experimental.pallas import tpu as pltpu
from jax.sharding import PartitionSpec as P

HEADS = 16
HEAD_DIM = 64
LAYERS = 2
MESH = pl.DeviceIdType.MESH


layer_eps = 1e-12
half_root = 0.7071067811865476
density_scale = 0.3989422804014327


class Place:
    def __init__(self, n, stride):
        position = lax.axis_index("dp")
        me = lax.div(position, stride) if stride > 1 else position
        self.me = me
        self.n = n
        self.depth = n // 4
        self.z = lax.div(me, 4)
        self.q = lax.rem(me, 4)
        low_bit = lax.rem(me, 2)
        high_bit = lax.rem(lax.div(me, 2), 2)
        self.step_x = 1 - 2 * low_bit
        self.step_y = 2 - 4 * high_bit
        self.dev_x = {"dp": position + self.step_x * stride}
        self.dev_y = {"dp": position + self.step_y * stride}
        self.position = position
        self.stride = stride
        self.dev_up = self.dev_plane(self.z + 1)
        self.dev_down = self.dev_plane(self.z - 1)
        self.can_up = self.z < self.depth - 1
        self.can_down = self.z > 0

    def dev_plane(self, zz):
        return {"dp": self.position + (zz - self.z) * 4 * self.stride}

    def planes(self, act, begin, end):
        down = begin > end

        def both(d):
            pl.when(self.z + d < self.depth)(lambda: act(self.z + d))
            pl.when(self.z - d >= 0)(lambda: act(self.z - d))

        def step(i, _):
            both(begin - i if down else begin + i)
            return 0

        if begin == 0:
            act(self.z)
            begin = 1
        count = 0 if begin == 1 and end == 0 and not down else abs(begin - max(end, 1)) + 1
        if count == 1:
            both(begin)
        elif count:
            lax.fori_loop(0, count, step, 0)
        if end == 0 and down:
            act(self.z)

    def cuts(self):
        far = self.depth - 1
        ends = [far * i // 3 for i in range(4)]
        return [(a + 1, b) for a, b in zip(ends[:-1], ends[1:])]

    def shard(self, zz, dx=False, dy=False):
        idx = zz * 4 + self.q
        if dx:
            idx = idx + self.step_x
        if dy:
            idx = idx + self.step_y
        return idx


def greet(place, straight):
    barrier = pltpu.get_barrier_semaphore()

    def call(dev):
        pl.semaphore_signal(barrier, inc=1, device_id=dev, device_id_type=MESH)

    call({"mp": 1 - lax.axis_index("mp")})
    call(place.dev_x)
    call(place.dev_y)
    if straight:
        for step in range(1, place.depth):
            call(place.dev_plane(lax.rem(place.z + step, place.depth)))
        count = 2 + place.depth
    else:
        pl.when(place.can_up)(lambda: call(place.dev_up))
        pl.when(place.can_down)(lambda: call(place.dev_down))
        count = 3 + place.can_up.astype(jnp.int32) + place.can_down.astype(jnp.int32)
    pl.semaphore_wait(barrier, count)


def remote(src, dst, send_sem, recv_sem, dev):
    return pltpu.make_async_remote_copy(
        src_ref=src, dst_ref=dst, send_sem=send_sem, recv_sem=recv_sem, device_id=dev, device_id_type=MESH
    )


class ColumnFirst:
    SENDS, RECVS = 6, 5

    def __init__(self, place, src, dst, start, size, cut, send, recv):
        self.p = place
        self.src = src.at[:, pl.ds(start, size)]
        self.dst = dst
        self.cols = pl.ds(start, size)
        self.sides = (pl.ds(start, cut), pl.ds(start + cut, size - cut))
        self.send = send
        self.recv = recv

    def at(self, idx):
        return self.dst.at[idx, :, self.cols]

    def _spread(self, src, zz):
        dst = self.at(self.p.shard(zz))
        return (
            remote(src, dst, self.send.at[2, zz], self.recv.at[1, zz], self.p.dev_x),
            remote(src, dst, self.send.at[3, zz], self.recv.at[2, zz], self.p.dev_y),
        )

    def _hop(self, src, zz, up):
        dst = self.at(self.p.shard(zz))
        dev = self.p.dev_up if up else self.p.dev_down
        return remote(src, dst, self.send.at[0 if up else 1, zz], self.recv.at[0, zz], dev)

    def _corner(self, idx_x, idx_y, zz):
        top, bottom = self.dst.at[idx_x, :, self.sides[0]], self.dst.at[idx_y, :, self.sides[1]]
        return (
            remote(top, top, self.send.at[5, zz], self.recv.at[3, zz], self.p.dev_y),
            remote(bottom, bottom, self.send.at[4, zz], self.recv.at[4, zz], self.p.dev_x),
        )

    def _corner_out(self, zz):
        return self._corner(self.p.shard(zz, dx=True), self.p.shard(zz, dy=True), zz)

    def _corner_in(self, zz):
        idx = self.p.shard(zz, dx=True, dy=True)
        return self._corner(idx, idx, zz)

    def first(self):
        z = self.p.z
        for copy in self._spread(self.src, z):
            copy.start()
        pl.when(self.p.can_up)(lambda: self._hop(self.src, z, True).start())
        pl.when(self.p.can_down)(lambda: self._hop(self.src, z, False).start())

    def pass_corner(self, zz):
        a, b = self._corner_out(zz)
        ix, iy = self.at(self.p.shard(zz, dx=True)), self.at(self.p.shard(zz, dy=True))
        remote(ix, ix, self.send.at[2, zz], self.recv.at[1, zz], self.p.dev_x).wait_recv()
        a.start()
        remote(iy, iy, self.send.at[3, zz], self.recv.at[2, zz], self.p.dev_y).wait_recv()
        b.start()

    def spread_plane(self, zz):
        src = self.at(self.p.shard(zz))
        self._hop(src, zz, True).wait_recv()
        pl.when((zz < self.p.z) & self.p.can_up)(lambda: self._hop(src, zz, True).start())
        pl.when((zz > self.p.z) & self.p.can_down)(lambda: self._hop(src, zz, False).start())
        for copy in self._spread(src, zz):
            copy.start()

    def ticks(self):
        cuts = [(0, 0)] + self.p.cuts()

        def step(now, before):
            self.p.planes(self.spread_plane, *now)
            self.p.planes(self.pass_corner, *before)

        steps = [functools.partial(step, now, before) for now, before in zip(cuts[1:], cuts[:-1])]
        return steps + [lambda: self.p.planes(self.pass_corner, *cuts[-1]), self.finish]

    def finish(self):
        z = self.p.z

        def drain(zz):
            for copy in self._corner_in(zz):
                copy.wait_recv()
            for copy in self._corner_out(zz):
                copy.wait_send()
            src = self.at(self.p.shard(zz))
            for copy in self._spread(src, zz):
                copy.wait_send()
            pl.when((zz <= z) & self.p.can_up)(lambda: self._hop(src, zz, True).wait_send())
            pl.when((zz >= z) & self.p.can_down)(lambda: self._hop(src, zz, False).wait_send())

        self.p.planes(drain, 0, self.p.depth - 1)


class SquareFirst:
    OWN, X, Y, CORNER = range(4)

    def __init__(self, place, src, dst, start, size, cut, send, recv, hop_send, hop_recv):
        self.p = place
        self.src = src.at[:, pl.ds(start, size)]
        self.dst = dst
        self.cols = pl.ds(start, size)
        self.sides = (pl.ds(start, cut), pl.ds(start + cut, size - cut))
        self.send = send
        self.recv = recv
        self.hop_send = hop_send
        self.hop_recv = hop_recv

    def _idx(self, who, zz):
        return self.p.shard(zz, dx=who in (1, 3), dy=who in (2, 3))

    def at(self, who, zz):
        return self.dst.at[self._idx(who, zz), :, self.cols]

    def _own(self):
        dst = self.at(0, self.p.z)
        return (
            remote(self.src, dst, self.send.at[0], self.recv.at[0], self.p.dev_x),
            remote(self.src, dst, self.send.at[1], self.recv.at[1], self.p.dev_y),
        )

    def _corner(self, idx_x, idx_y):
        top, bottom = self.dst.at[idx_x, :, self.sides[0]], self.dst.at[idx_y, :, self.sides[1]]
        return (
            remote(top, top, self.send.at[3], self.recv.at[2], self.p.dev_y),
            remote(bottom, bottom, self.send.at[2], self.recv.at[3], self.p.dev_x),
        )

    def _corner_out(self):
        return self._corner(self._idx(1, self.p.z), self._idx(2, self.p.z))

    def _corner_in(self):
        idx = self._idx(3, self.p.z)
        return self._corner(idx, idx)

    def _hop(self, src, who, zz, up):
        dev = self.p.dev_up if up else self.p.dev_down
        return remote(
            src, self.at(who, zz), self.hop_send.at[0 if up else 1, who, zz], self.hop_recv.at[who, zz], dev
        )

    def _leave(self, src, who):
        z = self.p.z
        pl.when(self.p.can_up)(lambda: self._hop(src, who, z, True).start())
        pl.when(self.p.can_down)(lambda: self._hop(src, who, z, False).start())

    def _take(self, who, far, near):
        def act(zz):
            src = self.at(who, zz)
            self._hop(src, who, zz, True).wait_recv()
            pl.when((zz < self.p.z) & self.p.can_up)(lambda: self._hop(src, who, zz, True).start())
            pl.when((zz > self.p.z) & self.p.can_down)(lambda: self._hop(src, who, zz, False).start())

        self.p.planes(act, far, near)

    def first(self):
        for copy in self._own():
            copy.start()
        self._leave(self.src, 0)

    def _cross(self):
        z = self.p.z
        a, b = self._corner_out()
        ix, iy = self.at(1, z), self.at(2, z)
        remote(ix, ix, self.send.at[0], self.recv.at[0], self.p.dev_x).wait_recv()
        a.start()
        self._leave(ix, 1)
        remote(iy, iy, self.send.at[1], self.recv.at[1], self.p.dev_y).wait_recv()
        b.start()
        self._leave(iy, 2)

    def _corner_done(self):
        for copy in self._corner_in():
            copy.wait_recv()
        self._leave(self.at(3, self.p.z), 3)

    def ticks(self):
        one, two, three = self.p.cuts()

        def first():
            self._cross()
            self._take(0, *one)

        def second():
            self._take(1, *one)
            self._take(2, *one)
            self._take(0, *two)
            self._corner_done()

        def third():
            self._take(1, *two)
            self._take(2, *two)
            self._take(0, *three)
            self._take(3, *one)

        def fourth():
            self._take(1, *three)
            self._take(2, *three)
            self._take(3, *two)

        def last():
            self._take(3, *three)
            self.finish()

        return [first, second, third, fourth, last]

    def finish(self):
        z = self.p.z
        for copy in self._own() + self._corner_out():
            copy.wait_send()

        def drain(zz):
            for who in range(4):
                src = self.at(who, zz)
                pl.when((zz <= z) & self.p.can_up)(lambda: self._hop(src, who, zz, True).wait_send())
                pl.when((zz >= z) & self.p.can_down)(lambda: self._hop(src, who, zz, False).wait_send())

        self.p.planes(drain, 0, self.p.depth - 1)


class Gather:
    def __init__(self, place, src, dst, turn, column_sems, square_sems, own_sem):
        tiles = src.shape[1] // 128
        square = max(1, tiles * 3 // 16)
        column = tiles - square
        cut = (column + turn) // 2
        self.src = src
        self.mine = dst.at[place.me]
        self.own_sem = own_sem
        self.jobs = [ColumnFirst(place, src, dst, 0, column * 128, max(1, cut) * 128, *column_sems)]
        if square > 1:
            square_cut = (square + 1 - turn) // 2
            self.jobs.append(
                SquareFirst(place, src, dst, column * 128, square * 128, square_cut * 128, *square_sems)
            )

    def _own(self):
        return pltpu.make_async_copy(self.src, self.mine, self.own_sem)

    def first(self):
        for job in self.jobs:
            job.first()
        self._own().start()

    def ticks(self):
        rows = list(zip(*[job.ticks() for job in self.jobs]))

        def step(row):
            for tick in row:
                tick()

        steps = [functools.partial(step, row) for row in rows]
        return steps[:-1] + [lambda: (steps[-1](), self._own().wait())]


class Scatter:
    def __init__(self, place, out, g, bufs, sems):
        self.p = place
        self.g = g
        self.out = out
        self.r1, self.r2, self.rz = bufs[:3]
        self.s1, self.v1, self.s2, self.v2, self.sz, self.vz = sems[:6]
        size = g.shape[2]
        self.main = self.r2.shape[3]
        self.main_cols = pl.ds(0, self.main)
        self.sides = self._halves(0, self.main)
        self.square = len(bufs) > 3
        if self.square:
            self.pz, self.p1, self.p2 = bufs[3:]
            self.tz, self.uz, self.t1, self.u1, self.t2, self.u2 = sems[6:]
            self.square_cols = pl.ds(self.main, size - self.main)
            self.square_sides = self._halves(self.main, size - self.main)

    def _halves(self, start, size):
        return pl.ds(start, size // 2), pl.ds(start + size // 2, size // 2)

    def _corner(self, zz):
        ic = self.p.shard(zz, dx=True, dy=True)
        top, bottom = self.sides
        return (
            remote(self.g.at[ic, :, top], self.r1.at[zz, 0], self.s1.at[zz, 0], self.v1.at[zz, 0], self.p.dev_y),
            remote(self.g.at[ic, :, bottom], self.r1.at[zz, 1], self.s1.at[zz, 1], self.v1.at[zz, 1], self.p.dev_x),
        )

    def _across(self, zz):
        to_x = self.g.at[self.p.shard(zz, dx=True), :, self.main_cols]
        to_y = self.g.at[self.p.shard(zz, dy=True), :, self.main_cols]
        return (
            remote(to_x, self.r2.at[zz, 0], self.s2.at[zz, 0], self.v2.at[zz, 0], self.p.dev_x),
            remote(to_y, self.r2.at[zz, 1], self.s2.at[zz, 1], self.v2.at[zz, 1], self.p.dev_y),
        )

    def _plane(self, zz):
        src, slot = self.g.at[self.p.shard(zz), :, self.main_cols], self.p.z
        return remote(src, self.rz.at[slot], self.sz.at[zz], self.vz.at[slot], self.p.dev_plane(zz))

    def _plane_in(self, zz):
        return remote(self.rz.at[zz], self.rz.at[zz], self.sz.at[zz], self.vz.at[zz], self.p.dev_plane(zz))

    def _square_plane(self, zz):
        src, slot = self.g.at[pl.ds(zz * 4, 4), :, self.square_cols], self.p.z
        return remote(src, self.pz.at[slot], self.tz.at[zz], self.uz.at[slot], self.p.dev_plane(zz))

    def _square_plane_in(self, zz):
        return remote(self.pz.at[zz], self.pz.at[zz], self.tz.at[zz], self.uz.at[zz], self.p.dev_plane(zz))

    def _square_corner(self):
        ic = self.p.shard(self.p.z, dx=True, dy=True)
        top, bottom = self.square_sides
        return (
            remote(self.g.at[ic, :, top], self.p1.at[0], self.t1.at[0], self.u1.at[0], self.p.dev_y),
            remote(self.g.at[ic, :, bottom], self.p1.at[1], self.t1.at[1], self.u1.at[1], self.p.dev_x),
        )

    def _square_across(self):
        to_x = self.g.at[self.p.shard(self.p.z, dx=True), :, self.square_cols]
        to_y = self.g.at[self.p.shard(self.p.z, dy=True), :, self.square_cols]
        return (
            remote(to_x, self.p2.at[0], self.t2.at[0], self.u2.at[0], self.p.dev_x),
            remote(to_y, self.p2.at[1], self.t2.at[1], self.u2.at[1], self.p.dev_y),
        )

    def _add(self, idx, cols, extra):
        at = (idx, slice(None), cols)
        total = self.g[at].astype(jnp.float32)
        for more in extra:
            total = total + more.astype(jnp.float32)
        self.g[at] = total.astype(self.g.dtype)

    def send_corner(self):
        def act(zz):
            for copy in self._corner(zz):
                copy.start()

        self.p.planes(act, self.p.depth - 1, 0)
        if self.square:
            self.p.planes(lambda zz: self._square_plane(zz).start(), self.p.depth - 1, 1)

    def send_across(self, far, near):
        def act(zz):
            a, b = self._corner(zz)
            to_x, to_y = self._across(zz)
            a.wait_recv()
            b.wait_recv()
            self._add(self.p.shard(zz, dx=True), self.sides[0], [self.r1[zz, 0]])
            self._add(self.p.shard(zz, dy=True), self.sides[1], [self.r1[zz, 1]])
            to_x.start()
            to_y.start()

        self.p.planes(act, far, near)

    def square_cross(self):
        z, depth = self.p.z, self.p.depth
        at = (pl.ds(z * 4, 4), slice(None), self.square_cols)

        def take(step, total):
            zz = lax.rem(z + step, depth)
            self._square_plane_in(zz).wait_recv()
            return total + self.pz[zz].astype(F32)

        total = lax.fori_loop(1, depth, take, self.g[at].astype(F32))
        for step in range(1, depth):
            self._square_plane(lax.rem(z + step, depth)).wait_send()
        self.g[at] = total.astype(self.g.dtype)
        for copy in self._square_corner():
            copy.start()

    def square_across(self):
        for copy in self._square_corner():
            copy.wait_recv()
        for i in range(2):
            idx = self.p.shard(self.p.z, dx=i == 0, dy=i == 1)
            self._add(idx, self.square_sides[i], [self.p1[i]])
        for copy in self._square_across():
            copy.start()

    def send_planes(self, far, near):
        def act(zz):
            for copy in self._across(zz):
                copy.wait_recv()
            self._add(self.p.shard(zz), self.main_cols, [self.r2[zz, 0], self.r2[zz, 1]])
            self._plane(zz).start()

        self.p.planes(act, far, near)

    def finish(self):
        z, out = self.p.z, self.out
        for copy in self._across(z):
            copy.wait_recv()
        total = self.g[self.p.me, :, self.main_cols].astype(F32)
        out[:, self.main_cols] = total + self.r2[z, 0].astype(F32) + self.r2[z, 1].astype(F32)

        def take(zz):
            self._plane_in(zz).wait_recv()
            out[:, self.main_cols] += self.rz[zz].astype(F32)
            self._plane(zz).wait_send()

        def drain(zz):
            for copy in self._corner(zz) + self._across(zz):
                copy.wait_send()

        self.p.planes(take, self.p.depth - 1, 1)
        self.p.planes(drain, self.p.depth - 1, 0)
        if self.square:
            for copy in self._square_across():
                copy.wait_recv()
            total = self.g[self.p.me, :, self.square_cols].astype(F32)
            out[:, self.square_cols] = total + self.p2[0].astype(F32) + self.p2[1].astype(F32)
            for copy in self._square_corner() + self._square_across():
                copy.wait_send()

    def crossings(self):
        steps = [lambda: self.send_across(self.p.depth - 1, 1), lambda: self.send_across(0, 0)]
        if self.square:
            steps[1] = lambda: (self.send_across(0, 0), self.square_cross())
        return steps

    def lines(self):
        steps = [functools.partial(self.send_planes, far, near) for near, far in reversed(self.p.cuts())]
        if self.square:
            begin = steps[0]
            steps[0] = lambda: (self.square_across(), begin())
        return steps


def scatter_scratch(n, rows, cols, dtype):
    dma = pltpu.SemaphoreType.DMA
    depth = n // 4
    square = cols // 1024 * 128
    main = cols - square
    bufs = [
        pltpu.VMEM((depth, 2, rows, main // 2), dtype),
        pltpu.VMEM((depth, 2, rows, main), dtype),
        pltpu.VMEM((depth, rows, main), dtype),
    ]
    sems = [dma((depth, 2)), dma((depth, 2)), dma((depth, 2)), dma((depth, 2)), dma((depth,)), dma((depth,))]
    if square:
        bufs += [
            pltpu.VMEM((depth, 4, rows, square), dtype),
            pltpu.VMEM((2, rows, square // 2), dtype),
            pltpu.VMEM((2, rows, square), dtype),
        ]
        sems += [dma((depth,)), dma((depth,)), dma((2,)), dma((2,)), dma((2,)), dma((2,))]
    return [pltpu.VMEM((n, rows, cols), dtype), bufs, sems]


VMEM, SMEM, ANY = pltpu.VMEM, pltpu.SMEM, pl.ANY


class Beside:
    def __init__(self):
        self.left = []
        self.done = set()

    def add(self, name, ticks):
        self.left += [(None, tick) for tick in ticks[:-1]] + [(name, ticks[-1])]

    def _next(self):
        name, tick = self.left.pop(0)
        self.done.add(name)
        return tick

    def __call__(self, count=1):
        for _ in range(count):
            if self.left:
                self._next()()

    def in_loop(self, i, steps):
        for step in steps:
            if self.left:
                self._at(i == step, self._next())

    def _at(self, now, tick):
        @pl.when(now)
        def _():
            tick()

    def until(self, name):
        while name not in self.done:
            self()

    def rest(self):
        self(len(self.left))


AHEAD = 3


def gather_stream(beside, jobs, along):
    ticks = [job.ticks() for job in jobs]
    side = along.ticks()

    def both(k):
        ticks[0][k]()
        side[k]()

    steps = [[functools.partial(both, k) for k in range(5)]] + ticks[1:]
    for slot in range(3 * len(jobs) + 2):
        for u, job_steps in enumerate(steps):
            k = slot - 3 * u
            if 0 <= k < 5:
                beside.add(("gathered", u) if k == 4 else None, [job_steps[k]])
            if k == 2 and u + AHEAD < len(jobs):
                beside.add(None, [jobs[u + AHEAD].first])


BAL_END, GIV_END, SHIFT_SEQ, SHIFT_POS, TURN = 0, 4, 8, 12, 16
LOW = jnp.bfloat16
F32 = jnp.float32


def plan_numbers(lengths, seq_order):
    seqs = range(4)
    length = [lengths[j] for j in seqs]
    order = [seq_order[j] for j in seqs]

    def picked(values, place):
        return sum(jnp.where(order[place] == j, values[j], 0) for j in seqs)

    def ends(values):
        return [sum(values[: j + 1]) for j in seqs]

    bal_len = [picked(length, i) for i in seqs]
    bal_end, giv_end = ends(bal_len), ends(length)
    bal_start = [end - size for end, size in zip(bal_end, bal_len)]
    giv_start = [end - size for end, size in zip(giv_end, length)]
    shift_seq = [sum(jnp.where(order[i] == j, bal_start[i], 0) for i in seqs) - giv_start[j] for j in seqs]
    shift_pos = [bal_start[i] - picked(giv_start, i) for i in seqs]
    return bal_end + giv_end + shift_seq + shift_pos + [bal_start[2]]


def places(ends, position, plan):
    seg = jnp.zeros_like(position)
    for j in range(4):
        seg = seg + (position >= plan[ends + j]).astype(jnp.int32)
    return seg


def turned(row, plan, total):
    position = row + plan[TURN]
    return jnp.where(position >= total, position - total, position)


def turned_back(position, plan, total):
    row = position - plan[TURN]
    return jnp.where(row < 0, row + total, row)


def shifted(position, seg, first, plan, sign):
    for j in range(4):
        position = position + sign * jnp.where(seg == j, plan[first + j], 0)
    return position


def column(start, count):
    return start + lax.broadcasted_iota(jnp.int32, (count, 1), 0)


def pick_matrix(index, keep, total):
    lanes = lax.broadcasted_iota(jnp.int32, (index.shape[0], total), 1)
    index = jnp.where(keep, index, -1)
    return jnp.where(lanes == index, 1.0, 0.0).astype(LOW)


def dot(a, b):
    return jnp.dot(a, b, preferred_element_type=F32)


def dot_nt(a, b):
    return lax.dot_general(a, b, (((1,), (1,)), ((), ())), preferred_element_type=F32)


def dot_tn(a, b):
    return lax.dot_general(a, b, (((0,), (0,)), ((), ())), preferred_element_type=F32)


def loop(count, act):
    def step(i, _):
        act(i)
        return 0

    lax.fori_loop(0, count, step, 0)


def part(i, size):
    return pl.ds(pl.multiple_of(i * size, size), size)


def inside(base, i, size):
    return pl.ds(pl.multiple_of(base + i * size, size), size)


def to_partner(src, dst, sems, slot):
    return remote(src, dst, sems.at[0, slot], sems.at[1, slot], {"mp": 1 - lax.axis_index("mp")})


def mean_rows(values):
    return jnp.mean(values, axis=-1, keepdims=True)


CHUNK = 64
TILE = 512
ROW_GAIN, ROW_HIDDEN, ROW_SQUARE, ROW_COUNT, VEC_ROWS = 12, 16, 20, 26, 32


def head_lanes(h, size):
    lanes = lax.broadcasted_iota(jnp.int32, (1, 2 * size), 1)
    mine = lanes < size if h == 0 else lanes >= size
    return jnp.where(mine, 1.0, 0.0).astype(LOW)


def gelu_pair(u):
    rise = 0.5 * (1.0 + lax.erf(u * half_root))
    slope = rise + u * density_scale * jnp.exp(-0.5 * u * u)
    return (u * rise).astype(LOW), slope.astype(LOW)


def norm_chunk(z, gain, shift):
    center = z - mean_rows(z)
    inv = lax.rsqrt(mean_rows(center * center) + layer_eps)
    unit = center * inv
    return unit * gain + shift, unit, inv


def norm_back_chunk(grad, unit, inv, gain):
    scaled = grad * gain
    inner = scaled - mean_rows(scaled) - unit * mean_rows(scaled * unit)
    return inner * inv


def turn_over(src, dst):
    step = 256

    def tile(i):
        dst[:, part(i, step)] = src[part(i, step), :].T

    loop(src.shape[0] // step, tile)


def weight_rows(weight, j, count, cols):
    span = weight.shape[1]
    return weight[part(j, count // span), :, cols].reshape(count, -1)


def weight_cols(weight, cols):
    return weight[:, :, cols].reshape(weight.shape[0] * weight.shape[1], -1)


class Moves:
    def __init__(self, sems):
        self.sems = sems
        self.slots = {}
        self.open = {}

    def start(self, name, src, dst):
        slot = self.slots.setdefault(name, len(self.slots))
        self.open[name] = lambda: pltpu.make_async_copy(src, dst, self.sems.at[slot])
        self.open[name]().start()

    def wait(self, *names):
        for name in names:
            if name in self.open:
                self.open.pop(name)().wait()

    def wait_all(self):
        self.wait(*list(self.open))


def forward_kernel(n, stride, sizes, *refs):
    rows, total, width, cols, hidden = sizes
    units = 3 * LAYERS
    refs = list(refs)

    def take(count):
        taken = refs[:count]
        del refs[:count]
        return taken

    lengths, seq_order, x, cot, w_qkv, w_out, w_in, w_back, biases, gains, hidden_bias = take(11)
    x_out, qm_out, probs_out, y_out, act_out, slope_out, unit_out, inv_out = take(8)
    weights = take(units)
    vec, squares, dh = take(3)
    first_src, small, small_all = take(3)
    xs, qm, probs, wa, wi, wb, y_all, act, slope, unit, inv, stream, yf, held, sent, got, bias = take(17)
    pair_sems, move_sems, probs_sems, gather_sems = take(4)
    core = lax.axis_index("mp")
    base, other = core * rows, (1 - core) * rows
    own = part(core, rows)
    half = total // 2
    size = HEAD_DIM
    pair = 2 * size
    scale = HEAD_DIM ** (-0.5)
    slabs = cols // pair
    place = Place(n, stride)
    *gather_sems, own_sems = gather_sems
    plan = plan_numbers(lengths, seq_order)

    def pack_first(layer):
        for i in range(3):
            first_src[layer, :, pl.ds(i * cols, cols)] = w_qkv[layer, i]
        first_src[layer, :, pl.ds(3 * cols, cols)] = w_out[layer]

    pack_first(0)
    small[...] = jnp.zeros_like(small)
    span = w_in.shape[1]
    for layer in range(LAYERS):
        for row, values in ((6 * layer, biases), (ROW_GAIN + 2 * layer, gains), (ROW_HIDDEN + 2 * layer, hidden_bias)):
            for i in range(6 if values is biases else values.shape[1]):
                value = values[i, layer : layer + 1] if values is biases else values[layer, i : i + 1]
                small[row + i : row + i + 1, pl.ds(0, span)] = value.astype(F32)
    shards = []
    for layer in range(LAYERS):
        shards += [first_src.at[layer], w_in.at[layer], w_back.at[layer]]
    jobs = []
    for u, (src, dst) in enumerate(zip(shards + [small], weights + [small_all])):
        sems = [sem.at[u] for sem in gather_sems]
        jobs.append(Gather(place, src, dst, u % 2, sems[:2], sems[2:], own_sems.at[u]))
    greet(place, False)
    little = jobs.pop()
    little.first()
    for job in jobs[:AHEAD]:
        job.first()
    beside = Beside()
    gather_stream(beside, jobs, little)
    moves = Moves(move_sems)
    for layer in range(1, LAYERS):
        pack_first(layer)

    def fetch(u, where):
        beside.until(("gathered", u))
        moves.start(where, weights[u], {"wa": wa, "wi": wi, "wb": wb}[where])

    x_given, cot_given = pl.ds(0, width), pl.ds(width, width)
    copies = [
        to_partner(x, act.at[own, x_given], pair_sems, 4),
        to_partner(cot, act.at[own, cot_given], pair_sems, 5),
    ]
    for copy in copies:
        copy.start()
    act[own, x_given] = x[...]
    act[own, cot_given] = cot[...]
    squares[...] = jnp.zeros_like(squares)
    for copy in copies:
        copy.wait()
    beside()

    def turn(i):
        index = turned(column(i * TILE, TILE), plan, total)
        picks = pick_matrix(index, index >= 0, total)
        xs[0, part(i, TILE), :] = dot(picks, act[:, x_given]).astype(LOW)

    loop(total // TILE, turn)
    moves.start("x", xs.at[0], x_out.at[0])
    beside()
    position = turned(column(base, rows), plan, total)
    seg = places(BAL_END, position, plan)
    target = shifted(position, seg, SHIFT_POS, plan, -1)
    dh[...] = dot(pick_matrix(target, seg < 4, total), act[:, cot_given]).astype(LOW)
    stream[...] = xs[0, own, :].astype(F32)
    fetch(0, "wa")

    per = 128 // span
    from_lane = lax.broadcasted_iota(jnp.int32, (128, 128), 0)
    to_lane = lax.broadcasted_iota(jnp.int32, (128, 128), 1)

    def spread(j):
        lanes = 0.0
        for i in range(per):
            shift = jnp.where(to_lane == from_lane + i * span, 1.0, 0.0).astype(LOW)
            lanes = lanes + dot(small_all[j * per + i, :, pl.ds(0, 128)].astype(LOW), shift)
        vec[:, part(j, 128)] = lanes

    loop(width // 128, spread)

    back = turned(column(half, half), plan, total)
    seg_k = places(BAL_END, back, plan)
    across = turned(half + lax.broadcasted_iota(jnp.int32, (1, half), 1), plan, total)
    seg_q = places(BAL_END, across, plan)

    def valid(i):
        return places(BAL_END, turned(column(base + i * CHUNK, CHUNK), plan, total), plan) < 4

    for layer in range(LAYERS):
        x_all = xs.at[layer % 2]
        next_all = xs.at[(layer + 1) % 2]
        row = 6 * layer
        gain = ROW_GAIN + 2 * layer
        head_span = part(core, cols)
        bias[...] = jnp.zeros_like(bias)
        bias[0:1, pl.ds(0, cols)] = vec[row : row + 1, head_span]
        bias[0:1, pl.ds(2 * cols, cols)] = vec[row + 1 : row + 2, head_span]
        moves.wait_all()

        def project(t):
            m, j = lax.div(t, 3), lax.rem(t, 3)
            acc = dot(x_all[part(m, TILE), :], weight_cols(wa, part(j, cols)))
            qm[part(m, TILE), part(j, cols)] = (acc + bias[0:1, part(j, cols)]).astype(LOW)
            beside.in_loop(t, [3])

        loop(3 * (total // TILE), project)
        beside()

        def probs_move(s):
            slot = s % 2 if isinstance(s, int) else lax.rem(s, 2)
            return pltpu.make_async_copy(probs.at[slot], probs_out.at[layer, s], probs_sems.at[slot])

        def slab(s):
            slot = lax.rem(s, 2)

            @pl.when(s >= 2)
            def _():
                probs_move(s - 2).wait()

            for b in range(2):
                at = pl.ds(b * half, half)
                q = qm[at, part(s, pair)]
                k = qm[at, inside(cols, s, pair)]
                v = qm[at, inside(2 * cols, s, pair)]
                mixed = []
                for h in range(2):
                    lanes = head_lanes(h, size)
                    scores = dot_nt(k, q * (lanes * scale))
                    if b == 1:
                        scores = jnp.where(seg_k == seg_q, scores, -1e30)
                    peak = jnp.max(scores, axis=0, keepdims=True)
                    powers = jnp.exp(scores - peak)
                    share = (powers * (1.0 / jnp.sum(powers, axis=0, keepdims=True))).astype(LOW)
                    probs[slot, b, pl.ds(h * half, half), :] = share
                    mixed.append(dot_tn(v, share)[h * size : (h + 1) * size, :])
                qm[at, inside(3 * cols, s, pair)] = jnp.concatenate(mixed, axis=0).T.astype(LOW)
            probs_move(s).start()
            beside.in_loop(s, range(slabs))

        loop(slabs, slab)
        moves.start("qm", qm, qm_out.at[layer])
        for s in range(max(slabs - 2, 0), slabs):
            probs_move(s).wait()

        def out_of(left, left_cols, right, right_cols, slot):
            def product(at, j):
                return dot_nt(left[at, left_cols], weight_rows(right, j, TILE, right_cols))

            def far(j):
                sent[slot, :, part(j, TILE)] = product(part(1 - core, rows), j).astype(LOW)

            loop(width // TILE, far)
            copy = to_partner(sent.at[slot], got.at[slot], pair_sems, slot)
            copy.start()
            beside()

            def near(j):
                held[:, part(j, TILE)] = product(own, j)

            loop(width // TILE, near)
            copy.wait()

        mix_cols = pl.ds(3 * cols, cols)
        out_of(qm, mix_cols, wa, mix_cols, 0)

        def first_norm(i):
            at = part(i, CHUNK)
            h = stream[at, :]
            a = held[at, :] + got[0, at, :].astype(F32) + vec[row + 2 : row + 3, :]
            ok = jnp.where(valid(i), 1.0, 0.0)
            squares[3 * layer : 3 * layer + 1, :] += jnp.sum(ok * h * h, axis=0, keepdims=True)
            squares[3 * layer + 1 : 3 * layer + 2, :] += jnp.sum(ok * a * a, axis=0, keepdims=True)
            y, z, r = norm_chunk(h + a, vec[gain : gain + 1, :], vec[row + 3 : row + 4, :])
            unit[0, at, :] = z
            inv[0, at, :] = jnp.broadcast_to(r, (CHUNK, 128))
            yf[at, :] = y
            y_all[inside(base, i, CHUNK), :] = y.astype(LOW)

        loop(rows // CHUNK, first_norm)
        y_copy = to_partner(y_all.at[own], y_all.at[own], pair_sems, 2)
        y_copy.start()
        fetch(3 * layer + 1, "wi")
        moves.wait("wi")

        def raise_rows(start, at_steps):
            def tile(t):
                at, col = pl.ds(pl.multiple_of(start, rows), rows), part(t, TILE)
                hidden_row = ROW_HIDDEN + 2 * layer + lax.div(t, width // TILE)
                shift = vec[pl.ds(hidden_row, 1), part(lax.rem(t, width // TILE), TILE)]
                value, grad = gelu_pair(dot(y_all[at, :], weight_cols(wi, col)) + shift)
                act[at, col] = value
                slope[at, col] = grad
                beside.in_loop(t, at_steps)

            loop(hidden // TILE, tile)

        raise_rows(base, [1, 3])
        y_copy.wait()
        moves.start("y", y_all, y_out.at[layer])
        raise_rows(other, [1, 3])
        moves.start("act", act, act_out.at[layer])
        moves.start("slope", slope, slope_out.at[layer])
        fetch(3 * layer + 2, "wb")
        moves.wait("wb")
        out_of(act, slice(None), wb, slice(None), 1)
        beside()

        def second_norm(i):
            at = part(i, CHUNK)
            f = held[at, :] + got[1, at, :].astype(F32) + vec[row + 4 : row + 5, :]
            ok = jnp.where(valid(i), 1.0, 0.0)
            squares[3 * layer + 2 : 3 * layer + 3, :] += jnp.sum(ok * f * f, axis=0, keepdims=True)
            h, z, r = norm_chunk(yf[at, :] + f, vec[gain + 1 : gain + 2, :], vec[row + 5 : row + 6, :])
            unit[1, at, :] = z
            inv[1, at, :] = jnp.broadcast_to(r, (CHUNK, 128))
            stream[at, :] = h
            next_all[inside(base, i, CHUNK), :] = h.astype(LOW)

        loop(rows // CHUNK, second_norm)
        moves.start("unit", unit, unit_out.at[layer])
        moves.start("inv", inv, inv_out.at[layer])
        if layer + 1 < LAYERS:
            pass_on = to_partner(next_all.at[own], next_all.at[own], pair_sems, 3)
            pass_on.start()
            fetch(3 * layer + 3, "wa")
            pass_on.wait()
            moves.start("x", next_all, x_out.at[layer + 1])
        else:
            pass_on = to_partner(next_all.at[own], x_out.at[LAYERS, own], pair_sems, 3)
            pass_on.start()
            moves.start("x", next_all.at[own], x_out.at[LAYERS, own])
            pass_on.wait()
    beside.rest()
    moves.wait_all()


def forward(lengths, seq_order, x, cot, weights, vectors, n, stride, part_count):
    rows, width = x.shape
    total = rows * part_count
    span, hidden = weights[2].shape[1:]
    cols = weights[0].shape[3]
    shape = jax.ShapeDtypeStruct
    units = 3 * LAYERS
    half = total // 2
    slabs = cols // (2 * HEAD_DIM)
    dma = pltpu.SemaphoreType.DMA
    depth = n // 4
    vmem, smem, far = [pl.BlockSpec(memory_space=where) for where in (VMEM, SMEM, ANY)]
    outs = [
        shape((LAYERS + 1, total, width), LOW),
        shape((LAYERS, total, 4 * cols), LOW),
        shape((LAYERS, slabs, 2, 2 * half, half), LOW),
        shape((LAYERS, total, width), LOW),
        shape((LAYERS, total, hidden), LOW),
        shape((LAYERS, total, hidden), LOW),
        shape((LAYERS, 2, rows, width), F32),
        shape((LAYERS, 2, rows, 128), F32),
    ]
    outs += [shape((n, span, hidden), LOW)] * units
    outs += [
        shape((VEC_ROWS, width), F32),
        shape((8, width), F32),
        shape((rows, width), LOW),
    ]
    results = pl.pallas_call(
        functools.partial(forward_kernel, n, stride, (rows, total, width, cols, hidden)),
        out_shape=outs,
        in_specs=[smem, smem, vmem, vmem, vmem, vmem, far, far, vmem, vmem, vmem],
        out_specs=[far] * (8 + units) + [vmem] * 3,
        scratch_shapes=[
            VMEM((LAYERS, span, hidden), LOW),
            VMEM((VEC_ROWS, 256), F32),
            VMEM((n, VEC_ROWS, 256), F32),
            VMEM((2, total, width), LOW),
            VMEM((total, 4 * cols), LOW),
            VMEM((2, 2, 2 * half, half), LOW),
            VMEM((n, span, hidden), LOW),
            VMEM((n, span, hidden), LOW),
            VMEM((n, span, hidden), LOW),
            VMEM((total, width), LOW),
            VMEM((total, hidden), LOW),
            VMEM((total, hidden), LOW),
            VMEM((2, rows, width), F32),
            VMEM((2, rows, 128), F32),
            VMEM((rows, width), F32),
            VMEM((rows, width), F32),
            VMEM((rows, width), F32),
            VMEM((2, rows, width), LOW),
            VMEM((2, rows, width), LOW),
            VMEM((8, 3 * cols), F32),
            dma((2, 6)),
            dma((12,)),
            dma((2,)),
            [
                dma((units + 1, ColumnFirst.SENDS, depth)),
                dma((units + 1, ColumnFirst.RECVS, depth)),
                dma((units + 1, 4)),
                dma((units + 1, 4)),
                dma((units + 1, 2, 4, depth)),
                dma((units + 1, 4, depth)),
                dma((units + 1,)),
            ],
        ],
        compiler_params=pltpu.CompilerParams(
            collective_id=0, has_side_effects=True, vmem_limit_bytes=62 << 20
        ),
        name="forward",
    )(lengths, seq_order, x, cot, *weights, *vectors)
    return results[:8], results[8 : 8 + units], results[8 + units :]


def backward_kernel(n, stride, slot_count, sizes, *refs):
    rows, total, width, cols, hidden = sizes
    units = 3 * LAYERS
    refs = list(refs)

    def take(count):
        taken = refs[:count]
        del refs[:count]
        return taken

    lengths, seq_order, vec, squares, dh_in = take(5)
    plan = plan_numbers(lengths, seq_order)
    x_far, qm_far, probs_far, y_far, act_far, slope_far, unit_far, inv_far = take(8)
    weights = take(units)
    output, input_grad, grad_qkv, grad_out, grad_in, grad_back = take(6)
    own_small, partner_small = take(2)
    w1, w2, h1, h2, n1, sides, flip, probs = take(8)
    unit_rows, inv, dz, dh, sent, got, grads, staged = take(8)
    pair_sems, move_sems, probs_sems, read_sem = take(4)
    slots = take(slot_count)
    (little_refs,) = take(1)
    core = lax.axis_index("mp")
    base, other = core * rows, (1 - core) * rows
    own = part(core, rows)
    half = total // 2
    size = HEAD_DIM
    pair = 2 * size
    scale = HEAD_DIM ** (-0.5)
    slabs = cols // pair
    span = width // n
    place = Place(n, stride)
    moves = Moves(move_sems)
    crossings, lines = Beside(), Beside()
    jobs = [Scatter(place, staged, *slots[u % slot_count]) for u in range(units)]
    little = Scatter(place, own_small, *little_refs)

    def load_norm(layer):
        moves.start("unit", unit_far.at[layer, 1], unit_rows)
        moves.start("inv", inv_far.at[layer], inv)

    def free(u):
        if u >= slot_count:
            end(u - slot_count)

    def cross(u):
        crossings.until(u)

    def line(u, stage):
        crossings.until(u)
        lines.until((u, stage))

    def end(u):
        crossings.until(u)
        lines.until(u)

    def summed(u):
        job = jobs[u]
        job.send_corner()

        layer = last - u // 3
        if u % 3 == 2:
            targets = [(job.out.at[:, pl.ds(i * cols, cols)], grad_qkv.at[layer, i]) for i in range(3)]
            targets.append((job.out.at[:, pl.ds(3 * cols, cols)], grad_out.at[layer]))
        else:
            targets = [(job.out, (grad_back, grad_in)[u % 3].at[layer])]
        names = ["staged%d" % i for i in range(4)]

        def leave():
            moves.wait(*names)
            job.finish()
            for name, target in zip(names, targets):
                moves.start(name, *target)

        crossings.add(u, job.crossings())
        for stage, tick in enumerate(job.lines()):
            lines.add((u, stage), [tick])
        lines.add(u, [leave])

    last = LAYERS - 1
    moves.start("dh", dh_in, sent)
    load_norm(last)
    moves.start("w2", weights[3 * last + 2], w2)
    moves.start("h2", slope_far.at[last], h2)
    moves.start("h1", act_far.at[last], h1)
    moves.start("w1", weights[3 * last + 1], w1)
    moves.start("n1", y_far.at[last], n1)
    greet(place, True)
    grads[...] = jnp.zeros_like(grads)
    moves.wait("dh")

    def widen(i):
        dh[part(i, CHUNK), :] = sent[part(i, CHUNK), :].astype(F32)

    loop(rows // CHUNK, widen)

    def add_sum(row, values, lanes=slice(None)):
        grads[row : row + 1, lanes] += jnp.sum(values, axis=0, keepdims=True)

    for layer in reversed(range(LAYERS)):
        row = 6 * layer
        gain = ROW_GAIN + 2 * layer
        unit = 3 * (last - layer)
        moves.wait("unit", "inv")

        def second_norm(i):
            at = part(i, CHUNK)
            grad, z = dh[at, :], unit_rows[at, :]
            add_sum(gain + 1, grad * z)
            add_sum(row + 5, grad)
            out = norm_back_chunk(grad, z, inv[1, at, 0:1], vec[gain + 1 : gain + 2, :])
            dz[at, :] = out
            df = out.astype(LOW)
            add_sum(row + 4, df.astype(F32))
            sides[inside(base, i, CHUNK), :] = df

        loop(rows // CHUNK, second_norm)
        moves.start("unit", unit_far.at[layer, 0], unit_rows)
        if unit:
            pl.semaphore_wait(read_sem, 1)
        df_copy = to_partner(sides.at[own], sides.at[own], pair_sems, 0)
        df_copy.start()
        moves.wait("w2", "h2")

        def hidden_rows(start):
            def tile(t):
                at, col = pl.ds(pl.multiple_of(start, rows), rows), part(t, TILE)
                grad = (dot(sides[at, :], weight_cols(w2, col)) * h2[at, col].astype(F32)).astype(LOW)
                h2[at, col] = grad
                hidden_row = ROW_HIDDEN + 2 * layer + lax.div(t, width // TILE)
                grads[pl.ds(hidden_row, 1), part(lax.rem(t, width // TILE), TILE)] += jnp.sum(
                    grad.astype(F32), axis=0, keepdims=True
                )

            loop(hidden // TILE, tile)

        hidden_rows(base)
        df_copy.wait()
        turn_over(sides, flip)
        shards = TILE // span

        def outer(g, right, right_cols, g_cols, count, step):
            def tile(t):
                m, j = lax.div(t, count), lax.rem(t, count)
                value = dot(flip[part(m, TILE), :], right[:, inside(right_cols, j, step)])
                g[part(m, shards), :, inside(g_cols, j, step)] = value.astype(LOW).reshape(shards, span, step)

            loop((width // TILE) * count, tile)

        moves.wait("h1")
        free(unit)
        outer(jobs[unit].g, h1, 0, 0, hidden // TILE, TILE)
        summed(unit)
        if unit:
            line(unit - 2, 0)
        moves.start("h1", qm_far.at[layer], h1)
        hidden_rows(other)
        moves.start("w2", weights[3 * layer], w2)
        moves.wait("w1")

        def product(at, left, left_cols, right, right_cols, j):
            return dot_nt(left[at, left_cols], weight_rows(right, j, TILE, right_cols))

        every = slice(None)

        def far(j):
            sent[:, part(j, TILE)] = product(part(1 - core, rows), h2, every, w1, every, j).astype(LOW)

        loop(width // TILE, far)
        dy_copy = to_partner(sent, got, pair_sems, 1)
        dy_copy.start()

        def near(j):
            dh[:, part(j, TILE)] = product(own, h2, every, w1, every, j)

        loop(width // TILE, near)
        if unit:
            line(unit - 2, 1)
        moves.wait("unit")
        dy_copy.wait()

        def first_norm(i):
            at = part(i, CHUNK)
            grad, z = dz[at, :] + dh[at, :] + got[at, :].astype(F32), unit_rows[at, :]
            add_sum(gain, grad * z)
            add_sum(row + 3, grad)
            out = norm_back_chunk(grad, z, inv[0, at, 0:1], vec[gain : gain + 1, :])
            dz[at, :] = out
            da = out.astype(LOW)
            add_sum(row + 2, da.astype(F32))
            sides[inside(base, i, CHUNK), :] = da

        loop(rows // CHUNK, first_norm)
        da_copy = to_partner(sides.at[own], sides.at[own], pair_sems, 2)
        da_copy.start()
        if layer:
            load_norm(layer - 1)
            moves.start("w1", weights[3 * layer - 2], w1)
        if unit:
            line(unit - 2, 2)
            cross(unit - 1)
        else:
            cross(unit)
        free(unit + 1)
        moves.wait("n1")
        turn_over(n1, flip)
        moves.start("n1", x_far.at[layer], n1)
        outer(jobs[unit + 1].g, h2, 0, 0, hidden // TILE, TILE)
        summed(unit + 1)
        da_copy.wait()
        moves.wait("w2", "h1")
        mix_cols = pl.ds(3 * cols, cols)

        def probs_move(s, b):
            return pltpu.make_async_copy(probs_far.at[layer, s, b], probs.at[b], probs_sems.at[b])

        for b in range(2):
            probs_move(0, b).start()

        def mix_grad(m):
            value = dot(sides[part(m, TILE), :], weight_cols(w2, mix_cols))
            h2[part(m, TILE), mix_cols] = value.astype(LOW)

        loop(total // TILE, mix_grad)

        def slab(s):
            for b in range(2):
                at = pl.ds(b * half, half)
                q = h1[at, part(s, pair)]
                k = h1[at, inside(cols, s, pair)]
                v = h1[at, inside(2 * cols, s, pair)]
                do = h2[at, inside(3 * cols, s, pair)]
                inner = (do.astype(F32) * h1[at, inside(3 * cols, s, pair)].astype(F32)).T
                probs_move(s, b).wait()
                dq, dk, dv = [], 0.0, 0.0
                for h in range(2):
                    lanes = head_lanes(h, size)
                    mine = do * lanes
                    share = probs[b, pl.ds(h * half, half), :]
                    rowsum = jnp.sum(inner[h * size : (h + 1) * size, :], axis=0, keepdims=True)
                    ds = (share.astype(F32) * (dot_nt(v, mine) - rowsum)).astype(LOW)
                    dk = dk + dot(ds, q * (lanes * scale))
                    dv = dv + dot(share, mine)
                    dq.append(dot_tn(k, ds)[h * size : (h + 1) * size, :])

                @pl.when(s + 1 < slabs)
                def _(b=b):
                    probs_move(s + 1, b).start()

                dq = (jnp.concatenate(dq, axis=0) * scale).T.astype(LOW)
                dk, dv = dk.astype(LOW), dv.astype(LOW)
                h2[at, part(s, pair)] = dq
                h2[at, inside(cols, s, pair)] = dk
                h2[at, inside(2 * cols, s, pair)] = dv
                lanes_here = inside(core * cols, s, pair)
                add_sum(row, dq.astype(F32), lanes_here)
                add_sum(row + 1, dv.astype(F32), lanes_here)
            if unit:
                crossings.in_loop(s, [0, 0])
            lines.in_loop(s, [1, 2, 3])

        loop(slabs, slab)
        qkv_cols = pl.ds(0, 3 * cols)

        def far_input(j):
            value = product(part(1 - core, rows), h2, qkv_cols, w2, qkv_cols, j)
            sent[:, part(j, TILE)] = value.astype(LOW)

        loop(width // TILE, far_input)
        dh_copy = to_partner(sent, got, pair_sems, 3)
        dh_copy.start()

        def near_input(j):
            at = part(j, TILE)
            dh[:, at] = dz[:, at] + product(own, h2, qkv_cols, w2, qkv_cols, j)

        loop(width // TILE, near_input)
        if layer:
            moves.start("w2", weights[3 * layer - 1], w2)
        cross(unit + 1)
        free(unit + 2)
        g = jobs[unit + 2].g
        turn_over(sides, flip)
        if layer:
            pl.semaphore_signal(
                read_sem, inc=1, device_id={"mp": 1 - core}, device_id_type=MESH
            )
        outer(g, h1, 3 * cols, 3 * cols, 1, cols)
        if layer:
            moves.start("h1", act_far.at[layer - 1], h1)
        moves.wait("n1")
        turn_over(n1, flip)
        moves.start("n1", y_far.at[layer - 1] if layer else x_far.at[LAYERS], n1)
        outer(g, h2, 0, 0, 3, cols)
        summed(unit + 2)
        if layer:
            moves.start("h2", slope_far.at[layer - 1], h2)
        dh_copy.wait()

        def add_got(i):
            dh[part(i, CHUNK), :] += got[part(i, CHUNK), :].astype(F32)

        loop(rows // CHUNK, add_got)

    totals = jnp.sum(squares[0 : 3 * LAYERS, :], axis=1, keepdims=True)
    grads[ROW_SQUARE : ROW_SQUARE + 3 * LAYERS, :] = jnp.broadcast_to(totals, (3 * LAYERS, width))
    count = jnp.full((1, width), plan[BAL_END + 3], jnp.int32).astype(F32)
    grads[ROW_COUNT : ROW_COUNT + 1, :] = count
    per = 128 // span
    little.g[...] = jnp.zeros_like(little.g)

    def cut(j):
        lanes = grads[:, part(j, 128)]
        for i in range(per):
            little.g[j * per + i, :, pl.ds(0, 128)] = lanes

    loop(width // 128, cut)
    little.send_corner()

    dh_copy = to_partner(dh, unit_rows, pair_sems, 0)
    dh_copy.start()
    line(units - 3, 2)
    step = rows // 4
    moves.wait("n1")

    def give(i):
        given = column(base + i * step, step)
        seg = places(GIV_END, given, plan)
        source = turned_back(shifted(given, seg, SHIFT_SEQ, plan, 1), plan, total)
        sent[part(i, step), :] = dot(pick_matrix(source, seg < 4, total), n1[...]).astype(LOW)

    loop(4, give)
    moves.start("output", sent, output)
    dh_copy.wait()
    low_cols = pl.ds(0, width)

    def split(i):
        for start, values in ((base, dh), (other, unit_rows)):
            value = values[part(i, CHUNK), :]
            top = value.astype(LOW)
            at = inside(start, i, CHUNK)
            sides[at, :] = top
            h1[at, low_cols] = (value - top.astype(F32)).astype(LOW)

    loop(rows // CHUNK, split)

    def turn_back(i):
        back = turned_back(column(base + i * step, step), plan, total)
        picks = pick_matrix(back, back >= 0, total)
        dz[part(i, step), :] = dot(picks, sides[...]) + dot(picks, h1[:, low_cols])

    loop(4, turn_back)
    moves.start("input_grad", dz, input_grad)
    little_ticks = little.crossings() + little.lines() + [little.finish]
    for tick in little_ticks[:2]:
        tick()
    end(units - 3)
    cross(units - 1)
    for tick in little_ticks[2:]:
        tick()
    swap = to_partner(own_small, partner_small, pair_sems, 1)
    swap.start()
    end(units - 1)
    swap.wait()
    moves.wait_all()


def backward(lengths, seq_order, vec, squares, dh, kept, weights, n, stride):
    rows, width = dh.shape
    total, hidden = kept[4].shape[1:]
    slot_count = 3 if n <= 16 else 2
    span = weights[0].shape[1]
    cols = kept[1].shape[2] // 4
    units = len(weights)
    half = total // 2
    shape = jax.ShapeDtypeStruct
    dma = pltpu.SemaphoreType.DMA
    vmem, smem, far = [pl.BlockSpec(memory_space=where) for where in (VMEM, SMEM, ANY)]
    outs = [shape((rows, width), LOW), shape((rows, width), F32)]
    outs += [
        shape((LAYERS, 3, span, cols), F32),
        shape((LAYERS, span, cols), F32),
        shape((LAYERS, span, hidden), F32),
        shape((LAYERS, span, hidden), F32),
    ]
    outs += [shape((VEC_ROWS, 256), F32)] * 2
    results = pl.pallas_call(
        functools.partial(backward_kernel, n, stride, slot_count, (rows, total, width, cols, hidden)),
        out_shape=outs,
        in_specs=[smem, smem, vmem, vmem] + [far] * (9 + units),
        out_specs=[far] * 6 + [vmem] * 2,
        scratch_shapes=[
            VMEM((n, span, hidden), LOW),
            VMEM((n, span, hidden), LOW),
            VMEM((total, hidden), LOW),
            VMEM((total, hidden), LOW),
            VMEM((total, width), LOW),
            VMEM((total, width), LOW),
            VMEM((width, total), LOW),
            VMEM((2, 2 * half, half), LOW),
            VMEM((rows, width), F32),
            VMEM((2, rows, 128), F32),
            VMEM((rows, width), F32),
            VMEM((rows, width), F32),
            VMEM((rows, width), LOW),
            VMEM((rows, width), LOW),
            VMEM((VEC_ROWS, width), F32),
            VMEM((span, hidden), F32),
            dma((2, 4)),
            dma((20,)),
            dma((2,)),
            pltpu.SemaphoreType.REGULAR,
        ]
        + [scatter_scratch(n, span, hidden, LOW)] * slot_count
        + [scatter_scratch(n, VEC_ROWS, 256, F32)],
        compiler_params=pltpu.CompilerParams(
            collective_id=1, has_side_effects=True, vmem_limit_bytes=63 << 20
        ),
        name="backward",
    )(lengths, seq_order, vec, squares, dh, *kept, *weights)
    return results[:2], results[2:6], results[6:]


def grouped(values, stride, own):
    total = values
    for step in range(1, stride):
        n = lax.axis_size("dp")
        pairs = [(i, i - i % stride + (i + step) % stride) for i in range(n)]
        total = total + lax.ppermute(values, "dp", pairs)
    return total


def body(
    inputs,
    cotangent,
    lengths,
    seq_order,
    w_qkv,
    w_out,
    w_in,
    w_back,
    biases,
    norm_gains,
    hidden_bias,
):
    devices = lax.axis_size("dp")
    part_count = lax.axis_size("mp")
    width = inputs.shape[1]
    span = biases.shape[2]
    cols = w_qkv.shape[3]
    stride = max(1, 16 // span)
    n = devices // stride
    place_here = lax.axis_index("dp")

    def shared(values, axis):
        if stride == 1:
            return values
        shape = list(values.shape)
        size = shape[axis]
        shape[axis] = size * stride
        start = lax.rem(place_here, stride) * size
        return grouped(lax.dynamic_update_slice_in_dim(jnp.zeros(shape, values.dtype), values, start, axis), stride, 0)

    turned_out, turned_back = jnp.swapaxes(w_out, 1, 2), jnp.swapaxes(w_back, 1, 2)
    weights = [shared(w_qkv, 2), shared(turned_out, 1), shared(w_in, 1), shared(turned_back, 1)]
    vectors = [shared(vector, 2) for vector in (jnp.swapaxes(biases, 0, 1), norm_gains, hidden_bias)]
    lengths, seq_order = lengths.reshape(-1), seq_order.reshape(-1)
    kept, gathered, (vec, squares, dh) = forward(
        lengths, seq_order, inputs, cotangent, weights, vectors, n, stride, part_count
    )
    (output, input_grad), sums, (own_small, partner_small) = backward(
        lengths, seq_order, vec, squares, dh, kept, gathered, n, stride
    )

    if stride > 1:
        start = lax.rem(place_here, stride) * span
        sums = [lax.dynamic_slice_in_dim(grouped(sum_, stride, 0), start, span, sum_.ndim - 2) for sum_ in sums]
        own_small, partner_small = grouped(own_small, stride, 0), grouped(partner_small, stride, 0)
    both = own_small + partner_small
    lane = lax.rem(place_here, 128 // span) * span

    def lanes(values):
        return lax.dynamic_slice_in_dim(values, lane, span, 1)

    grad_biases = lanes(both[:ROW_GAIN]).reshape(biases.shape)
    grad_gains = lanes(both[ROW_GAIN:ROW_HIDDEN]).reshape(norm_gains.shape)
    grad_hidden_bias = lanes(own_small[ROW_HIDDEN:ROW_SQUARE]).reshape(hidden_bias.shape)
    valid_count = both[ROW_COUNT, 0] / part_count
    rms = jnp.sqrt(both[ROW_SQUARE:ROW_COUNT, 0] / (valid_count * width)).reshape(LAYERS, 3)

    grad_qkv, grad_out, grad_in, grad_back = sums
    grad_out, grad_back = jnp.swapaxes(grad_out, 1, 2), jnp.swapaxes(grad_back, 1, 2)
    return (
        output,
        input_grad,
        grad_qkv,
        grad_out,
        grad_in,
        grad_back,
        grad_biases,
        grad_gains,
        grad_hidden_bias,
        rms,
    )


def solution(mesh):
    in_specs = (
        P(("dp", "mp"), None),
        P(("dp", "mp"), None),
        P("dp", None),
        P("dp", None),
        P(None, None, "dp", "mp"),
        P(None, "mp", "dp"),
        P(None, "dp", "mp"),
        P(None, "mp", "dp"),
        P(None, None, "dp"),
        P(None, None, "dp"),
        P(None, "mp", "dp"),
    )
    out_specs = (
        P(("dp", "mp"), None),
        P(("dp", "mp"), None),
        P(None, None, "dp", "mp"),
        P(None, "mp", "dp"),
        P(None, "dp", "mp"),
        P(None, "mp", "dp"),
        P(None, None, "dp"),
        P(None, None, "dp"),
        P(None, "mp", "dp"),
        P(),
    )
    return jax.shard_map(body, mesh=mesh, in_specs=in_specs, out_specs=out_specs, check_vma=False)
```

time: 2520 us -> 490 us (0.19)
  waiting for transfers between devices: 1560 us -> 0 us
  Pallas kernels: 0 us -> 470 us
  matrix products: 345 us -> 0 us
  blocking collectives: 299 us -> 0 us
  other arithmetic: 154 us -> 0.99 us
  local copies, waits for them, and re-layouts: 135 us -> 12.3 us
    reduce_scatter x14 -> x0, waiting for transfers between devices: 858 us -> none  [the longest x2 363 us: body(): lax.psum_scatter(mats[2], 'dp', scatter_dimension=0, tiled=True)]
    pallas_call x0 -> x2, Pallas kernels: none -> 470 us  [the longest x1 242 us: backward(): pl.pallas_call(functools.partial(backward_kernel, n, stride, slot_count,...]
    unnamed x38 -> x0, waiting for transfers between devices: 470 us -> none
    dot_general x36 -> x0, matrix products: 345 us -> none  [the longest x6 47 us: matmul(): return jnp.dot(left_mat, right_mat, preferred_element_type=jnp.float32)]
    all_gather x6 -> x0, blocking collectives: 256 us -> none  [the longest x2 90.5 us: fetch_forward(): lax.all_gather(biases[layer_idx], 'dp', axis=1, tiled=True)]
    all_gather x18 -> x0, waiting for transfers between devices: 236 us -> none  [the longest x2 115 us: fetch_forward(): lax.all_gather(w_back[layer_idx], 'dp', axis=1, tiled=True)]
    reduce_sum x27 -> x0, other arithmetic: 70.7 us -> none  [the longest x2 26.1 us: attend(): totals = jnp.sum(shifted, axis=-1, keepdims=True)]
    convert_element_type x9 -> x0, other arithmetic: 66 us -> none  [the longest x2 57 us: attend_back(): grad_scores = (probs * (grad_probs - inner_sum)).astype(jnp.bfloat16)]
  transfers between devices with their start and end apart: 35 -> 0, of which waited for: 23 -> 0; matrix products, arithmetic and copies ran while one was open for 17% -> 0% of each run, Pallas kernels for 0% -> 0%
where the time goes in v1:
time: 490 us; the launch traced here: 485 us
  Pallas kernels  470 us (96%)
  local copies, waits for them, and re-layouts  12.3 us (3%)
    pallas_call x1, Pallas kernels, backward(): pl.pallas_call(functools.partial(backward_kernel, n, stride, slot_count,...  242 us
    pallas_call x1, Pallas kernels, forward(): pl.pallas_call(functools.partial(forward_kernel, n, stride, (rows, total,...  228 us

profile of v1, /device:TPU:0, one launch (start us, length us, event | category | flops | bytes accessed | tf_op | source)
XLA Modules:
  0.0 484.7 jit_solution(3053452336592244318)
XLA Ops:
  0.6 228.0 %forward.1 = (bf16[3,1024,1024]{2,1,0:T(8,128)(2,1)}, bf16[2,1024,2048]{2,1,0:T(8,128)(2,1)}, bf16[2,4,2,1024,512]{4,3,2,1,0:T(8,128)(2,1)}, bf16[2,1024,1024]{2...) custom-call(s32[4]{0:T(128)} %bitcast.17, ...), custom_call_target="tpu_custom_call" | custom-call | tf_op jit(solution)/shard_map/forward/pallas_call | solution.py:1063
  228.7 241.8 %backward.1 = (bf16[512,1024]{1,0:T(8,128)(2,1)}, f32[512,1024]{1,0:T(8,128)}, f32[2,3,64,512]{3,2,1,0:T(8,128)}, f32[2,64,512]{2,1,0:T(8,128)}, f32[2,64,2048]{...) custom-call(s32[4]{0:T(128)} %bitcast.18, s32[4]{0:T(128)} %bitcast.20, ...), custom_call_target="tpu_custom_call" | custom-call | tf_op jit(solution)/shard_map/backward/pallas_call | solution.py:1495
  470.5 0.0 copy-start.2
  470.5 0.0 copy-start.3
  470.5 0.9 add.8
  471.3 0.5 slice.23
  472.5 0.1 fusion.1
  472.6 0.7 sqrt.8
  473.3 0.7 slice.17
  474.0 0.7 constant_dynamic-slice_fusion
  474.6 0.1 constant_dynamic-slice_fusion.2
  474.7 0.6 copy.21
  475.3 0.0 copy-start.1
  475.3 2.4 copy.28
  477.7 0.0 copy-start
  477.7 3.2 copy.29
  480.9 0.0 copy-done.2
  480.9 0.9 copy.30
  481.8 0.0 copy-done.3
  481.8 0.7 copy.31
  482.5 0.0 copy-done.1
  482.5 1.0 copy.32
  483.5 0.0 copy-done
  483.5 1.0 copy.33
  (3 shorter events, 0.0 us)
Async XLA Ops:
  470.5 10.5 %copy-start.2 = (f32[2,3,64,512]{3,2,1,0:T(8,128)S(1)}, f32[2,3,64,512]{3,2,1,0:T(8,128)}, u32[]{:S(2)}) copy-start(f32[2,3,64,512]{3,2,1,0:T(8,128)} %get-tuple-element.84) | copy-start | bytes 2359300
  470.5 11.3 %copy-start.3 = (f32[2,64,512]{2,1,0:T(8,128)S(1)}, f32[2,64,512]{2,1,0:T(8,128)}, u32[]{:S(2)}) copy-start(f32[2,64,512]{2,1,0:T(8,128)} %get-tuple-element.55) | copy-start | bytes 786436
  475.3 7.2 %copy-start.1 = (f32[2,64,2048]{2,1,0:T(8,128)S(1)}, f32[2,64,2048]{2,1,0:T(8,128)}, u32[]{:S(2)}) copy-start(f32[2,64,2048]{2,1,0:T(8,128)} %get-tuple-element.86) | copy-start | bytes 3145732
  477.7 5.8 %copy-start = (f32[2,64,2048]{2,1,0:T(8,128)S(1)}, f32[2,64,2048]{2,1,0:T(8,128)}, u32[]{:S(2)}) copy-start(f32[2,64,2048]{2,1,0:T(8,128)} %get-tuple-element.57) | copy-start | bytes 3145732

commit v2 on v1

--- a/solution.py
+++ b/solution.py
@@ -180,11 +180,16 @@
         return steps + [lambda: self.p.planes(self.pass_corner, *cuts[-1]), self.finish]
 
     def finish(self):
-        z = self.p.z
-
-        def drain(zz):
+        def take(zz):
             for copy in self._corner_in(zz):
                 copy.wait_recv()
+
+        self.p.planes(take, 0, self.p.depth - 1)
+
+    def drain(self):
+        z = self.p.z
+
+        def drain(zz):
             for copy in self._corner_out(zz):
                 copy.wait_send()
             src = self.at(self.p.shard(zz))
@@ -302,13 +307,9 @@
             self._take(2, *three)
             self._take(3, *two)
 
-        def last():
-            self._take(3, *three)
-            self.finish()
-
-        return [first, second, third, fourth, last]
-
-    def finish(self):
+        return [first, second, third, fourth, lambda: self._take(3, *three)]
+
+    def drain(self):
         z = self.p.z
         for copy in self._own() + self._corner_out():
             copy.wait_send()
@@ -355,6 +356,10 @@
 
         steps = [functools.partial(step, row) for row in rows]
         return steps[:-1] + [lambda: (steps[-1](), self._own().wait())]
+
+    def drain(self):
+        for job in self.jobs:
+            job.drain()
 
 
 class Scatter:
@@ -995,7 +1000,7 @@
         raise_rows(base, [1, 3])
         y_copy.wait()
         moves.start("y", y_all, y_out.at[layer])
-        raise_rows(other, [1, 3])
+        raise_rows(other, [1, 3] if layer + 1 < LAYERS else [3])
         moves.start("act", act, act_out.at[layer])
         moves.start("slope", slope, slope_out.at[layer])
         fetch(3 * layer + 2, "wb")
@@ -1029,6 +1034,8 @@
             moves.start("x", next_all.at[own], x_out.at[LAYERS, own])
             pass_on.wait()
     beside.rest()
+    for job in [little] + jobs:
+        job.drain()
     moves.wait_all()
 
 

time: 490 us -> 490 us (level)
  no operation moved by 1% of the time
where the time goes in v2:
time: 490 us; the launch traced here: 485 us
  Pallas kernels  470 us (96%)
  local copies, waits for them, and re-layouts  12.3 us (3%)
    pallas_call x1, Pallas kernels, backward(): pl.pallas_call(functools.partial(backward_kernel, n, stride, slot_count,...  241 us
    pallas_call x1, Pallas kernels, forward(): pl.pallas_call(functools.partial(forward_kernel, n, stride, (rows, total,...  229 us

profile of v2, /device:TPU:0, one launch (start us, length us, event | category | flops | bytes accessed | tf_op | source)
XLA Modules:
  0.0 485.1 jit_solution(12757888222477814330)
XLA Ops:
  0.6 229.1 %forward.1 = (bf16[3,1024,1024]{2,1,0:T(8,128)(2,1)}, bf16[2,1024,2048]{2,1,0:T(8,128)(2,1)}, bf16[2,4,2,1024,512]{4,3,2,1,0:T(8,128)(2,1)}, bf16[2,1024,1024]{2...) custom-call(s32[4]{0:T(128)} %bitcast.17, ...), custom_call_target="tpu_custom_call" | custom-call | tf_op jit(solution)/shard_map/forward/pallas_call | solution.py:1070
  229.8 241.1 %backward.1 = (bf16[512,1024]{1,0:T(8,128)(2,1)}, f32[512,1024]{1,0:T(8,128)}, f32[2,3,64,512]{3,2,1,0:T(8,128)}, f32[2,64,512]{2,1,0:T(8,128)}, f32[2,64,2048]{...) custom-call(s32[4]{0:T(128)} %bitcast.18, s32[4]{0:T(128)} %bitcast.20, ...), custom_call_target="tpu_custom_call" | custom-call | tf_op jit(solution)/shard_map/backward/pallas_call | solution.py:1502
  470.9 0.0 copy-start.2
  470.9 0.0 copy-start.3
  470.9 0.9 add.8
  471.8 0.5 slice.23
  472.9 0.1 fusion.1
  473.1 0.7 sqrt.8
  473.7 0.7 slice.17
  474.4 0.7 constant_dynamic-slice_fusion
  475.1 0.1 constant_dynamic-slice_fusion.2
  475.2 0.6 copy.21
  475.8 0.0 copy-start.1
  475.8 2.4 copy.28
  478.1 0.0 copy-start
  478.1 3.2 copy.29
  481.4 0.0 copy-done.2
  481.4 0.9 copy.30
  482.2 0.0 copy-done.3
  482.2 0.7 copy.31
  483.0 0.0 copy-done.1
  483.0 1.0 copy.32
  483.9 0.0 copy-done
  483.9 1.0 copy.33
  (3 shorter events, 0.0 us)
Async XLA Ops:
  470.9 10.5 %copy-start.2 = (f32[2,3,64,512]{3,2,1,0:T(8,128)S(1)}, f32[2,3,64,512]{3,2,1,0:T(8,128)}, u32[]{:S(2)}) copy-start(f32[2,3,64,512]{3,2,1,0:T(8,128)} %get-tuple-element.84) | copy-start | bytes 2359300
  470.9 11.3 %copy-start.3 = (f32[2,64,512]{2,1,0:T(8,128)S(1)}, f32[2,64,512]{2,1,0:T(8,128)}, u32[]{:S(2)}) copy-start(f32[2,64,512]{2,1,0:T(8,128)} %get-tuple-element.55) | copy-start | bytes 786436
  475.8 7.2 %copy-start.1 = (f32[2,64,2048]{2,1,0:T(8,128)S(1)}, f32[2,64,2048]{2,1,0:T(8,128)}, u32[]{:S(2)}) copy-start(f32[2,64,2048]{2,1,0:T(8,128)} %get-tuple-element.86) | copy-start | bytes 3145732
  478.1 5.8 %copy-start = (f32[2,64,2048]{2,1,0:T(8,128)S(1)}, f32[2,64,2048]{2,1,0:T(8,128)}, u32[]{:S(2)}) copy-start(f32[2,64,2048]{2,1,0:T(8,128)} %get-tuple-element.57) | copy-start | bytes 3145732
